TPU v7x, 32 devices: a whole 2x2x4 slice. The times are simulated.
32 devices in a mesh: state: 4 (over z), tile: 8 (over y, x, core).
Axes of the slice: x: 2, y: 2, z: 4, core: 2. Of those that a mesh axis runs over, the one named last changes fastest.
Arguments:
- bands: bfloat16 [4, 240, 131072], P('state', None, 'tile')
- block_slot: int32 [4, 1024], P('state', 'tile'), may hold values from 0 to 7
- tile_counties: int32 [4, 64], P('state', 'tile'), may hold values from 0 to 95, as said below
- county_place: int32 [4, 96], P('state'), may hold values from 0 to 95, as said below
- label: int32 [4, 96], P('state', 'tile'), may hold values from -200 to 200
- w_first: bfloat16 [64, 240], replicated, may hold values from -0.375 to 0.375
- taps: float32 [3, 64], replicated, may hold values from -2 to 2
- w_second: bfloat16 [128, 64], replicated, may hold values from -0.75 to 0.75
- w_third: bfloat16 [128, 128], replicated, may hold values from -0.5 to 0.5
- w_head: bfloat16 [128], replicated, may hold values from -0.5 to 0.5
Outputs:
- county_mean: float32 [4, 96], P('state', 'tile')
- weight_grads: float32 [40256], replicated
Inputs may be any that keep to these rules, and one draw needn't show every extreme that they name: `county_place`: each row is an ordering of the counties of one state region; the county at place p is owned by tile index p // 12 of that region. `tile_counties`: tile t's list names counties of its own state region owned by tile indices t, t + 1, ..., t + 4 - 1 (mod the tile axis's size); at most 4 entries of a list are owned by one tile index, and exactly 4 by t itself.
All inputs are finite; a program needn't handle non-finite values.
Results may differ from a plain program's by a relative error of at most 0.00064.
Values sent between devices are 32-bit elements; how exact they have to be, the bound alone decides.
A program may use at most 128 MiB of HBM per device.

v0:
```python
import jax
import jax.numpy as jnp
from jax import lax
from jax.sharding import PartitionSpec as P

MOST = 4
REACH = 4


def from_behind(value, axis, by):
    peers = lax.axis_size(axis)
    return lax.ppermute(value, axis, [(i, (i + by) % peers) for i in range(peers)])


def silu_parts(value):
    sig = jax.nn.sigmoid(value)
    return (value * sig, sig * (1.0 + value * (1.0 - sig)))


def along_rows(field, weights, row_len):
    chans, count = field.shape
    grid = field.reshape(chans, count // row_len, row_len)
    padded = jnp.pad(grid, ((0, 0), (0, 0), (1, 1)))
    out = (
        weights[0][:, None, None] * padded[:, :, :-2]
        + weights[1][:, None, None] * grid
        + weights[2][:, None, None] * padded[:, :, 2:]
    )
    return out.reshape(chans, count)


def tap_grads(field, upstream, row_len):
    chans, count = field.shape
    grid = field.reshape(chans, count // row_len, row_len)
    padded = jnp.pad(grid, ((0, 0), (0, 0), (1, 1)))
    above = upstream.reshape(grid.shape)
    return jnp.stack(
        [
            jnp.sum(above * padded[:, :, :-2], axis=(1, 2)),
            jnp.sum(above * grid, axis=(1, 2)),
            jnp.sum(above * padded[:, :, 2:], axis=(1, 2)),
        ]
    )


def contract_last(left, right):
    return lax.dot_general(
        left, right, (((1,), (1,)), ((), ())), preferred_element_type=jnp.float32
    )


def contract_first(left, right):
    return lax.dot_general(
        left, right, (((0,), (0,)), ((), ())), preferred_element_type=jnp.float32
    )


def forward(pixels, w_first, taps, w_second, w_third, w_head, row_len):
    h_one = jnp.dot(w_first, pixels, preferred_element_type=jnp.float32)
    s_one = along_rows(h_one, taps, row_len)
    a_one = silu_parts(s_one)[0].astype(jnp.bfloat16)
    h_two = jnp.dot(w_second, a_one, preferred_element_type=jnp.float32)
    a_two = silu_parts(h_two)[0].astype(jnp.bfloat16)
    h_three = jnp.dot(w_third, a_two, preferred_element_type=jnp.float32)
    a_three = (silu_parts(h_three)[0] + a_two.astype(jnp.float32)).astype(jnp.bfloat16)
    yhat = jnp.dot(w_head, a_three, preferred_element_type=jnp.float32)
    return (h_one, s_one, a_one, h_two, a_two, h_three, a_three, yhat)


def backward(pixels, saved, taps, w_second, w_third, w_head, cotangent, row_len):
    h_one, s_one, a_one, h_two, a_two, h_three, a_three, yhat = saved
    grad_in = cotangent.astype(jnp.bfloat16)
    d_head = jnp.dot(a_three, grad_in, preferred_element_type=jnp.float32)
    d_a3 = w_head.astype(jnp.float32)[:, None] * grad_in.astype(jnp.float32)[None, :]
    d_h3 = (d_a3 * silu_parts(h_three)[1]).astype(jnp.bfloat16)
    d_third = contract_last(d_h3, a_two)
    d_a2 = contract_first(w_third, d_h3) + d_a3
    d_h2 = (d_a2 * silu_parts(h_two)[1]).astype(jnp.bfloat16)
    d_second = contract_last(d_h2, a_one)
    d_a1 = contract_first(w_second, d_h2)
    d_s1 = d_a1 * silu_parts(s_one)[1]
    d_taps = tap_grads(h_one, d_s1, row_len)
    d_h1 = along_rows(d_s1, jnp.stack([taps[2], taps[1], taps[0]]), row_len).astype(jnp.bfloat16)
    d_first = contract_last(d_h1, pixels)
    return jnp.concatenate(
        [d_first.reshape(-1), d_taps.reshape(-1), d_second.reshape(-1), d_third.reshape(-1), d_head]
    )


def slot_stats(yhat, slots, slot_count):
    blocks = slots.shape[0]
    row_len = yhat.shape[0] // blocks
    member = (slots[None, :] == jnp.arange(slot_count, dtype=jnp.int32)[:, None]).astype(
        jnp.float32
    )
    block_sums = jnp.sum(yhat.reshape(blocks, row_len), axis=1)
    return (
        jnp.sum(member * block_sums[None, :], axis=1),
        jnp.sum(member, axis=1) * row_len,
        member,
    )


def place_of(counties, table):
    hits = counties[:, None] == jnp.arange(table.shape[0], dtype=jnp.int32)[None, :]
    return jnp.sum(jnp.where(hits, table[None, :], 0), axis=1)


def judge(sums, counts, labels, devices):
    denom = jnp.maximum(counts, 1.0)
    mean = sums / denom
    live = (counts > 0.5).astype(jnp.float32)
    target = labels.astype(jnp.float32) * 0.01
    return (mean, live * 2.0 * (mean - target) / (devices * denom))


def pixel_cotangent(member, slot_adjoint, row_len):
    block_adjoint = jnp.sum(member * slot_adjoint[:, None], axis=0)
    return jnp.broadcast_to(block_adjoint[:, None], (block_adjoint.shape[0], row_len)).reshape(-1)


def settle(sums, counts, codes, labels, devices):
    flat_codes = codes.reshape(-1)
    owned = jnp.arange(1, labels.shape[0] + 1, dtype=jnp.int32).astype(jnp.float32)
    hit = (flat_codes[:, None] == owned[None, :]).astype(jnp.float32)
    total = jnp.sum(hit * sums.reshape(-1)[:, None], axis=0)
    number = jnp.sum(hit * counts.reshape(-1)[:, None], axis=0)
    mean, adjoint = judge(total, number, labels, devices)
    back = jnp.sum(hit * adjoint[None, :], axis=1).reshape(codes.shape)
    return (mean, back)


def packed(select, values, rows):
    return jnp.sum(select * values[:, None], axis=0).reshape(rows, -1)


def on_device(
    bands, block_slot, tile_counties, county_place, label, w_first, taps, w_second, w_third, w_head
):
    pixels = bands[0]
    slots = block_slot[0]
    row_len = pixels.shape[1] // slots.shape[0]
    slot_total = tile_counties.shape[1]
    saved = forward(pixels, w_first, taps, w_second, w_third, w_head, row_len)
    slot_sums, slot_counts, member = slot_stats(saved[-1], slots, slot_total)
    table = county_place[0]
    place = place_of(tile_counties[0], table)
    labels_mine = label[0]
    cty_dev = labels_mine.shape[0]
    n_tile = lax.axis_size("tile")
    devices = float(lax.axis_size("state") * n_tile)
    owner = place // cty_dev
    local_code = (place % cty_dev + 1).astype(jnp.float32)
    order = jnp.arange(slot_total, dtype=jnp.int32)
    rank = jnp.sum(
        ((owner[:, None] == owner[None, :]) & (order[None, :] < order[:, None])).astype(jnp.int32),
        axis=1,
    )
    me = lax.axis_index("tile")
    position = (owner - me) % n_tile * MOST + rank
    select = (position[:, None] == jnp.arange(REACH * MOST, dtype=jnp.int32)[None, :]).astype(
        jnp.float32
    )
    out_sums = packed(select, slot_sums, REACH)
    out_counts = packed(select, slot_counts, REACH)
    out_codes = packed(select, local_code, REACH)
    got_sums, got_counts, got_codes = ([], [], [])
    for step in range(REACH):
        if step == 0:
            piece = (out_sums[0], out_counts[0], out_codes[0])
        else:
            piece = from_behind((out_sums[step], out_counts[step], out_codes[step]), "tile", step)
        got_sums.append(piece[0])
        got_counts.append(piece[1])
        got_codes.append(piece[2])
    county_mean, back = settle(
        jnp.stack(got_sums), jnp.stack(got_counts), jnp.stack(got_codes), labels_mine, devices
    )
    rows = []
    for step in range(REACH):
        if step == 0:
            rows.append(back[0])
        else:
            rows.append(from_behind(back[step], "tile", -step))
    returned = jnp.stack(rows).reshape(-1)
    slot_adjoint = jnp.sum(select * returned[None, :], axis=1)
    cotangent = pixel_cotangent(member, slot_adjoint, row_len)
    local_grads = backward(pixels, saved, taps, w_second, w_third, w_head, cotangent, row_len)
    share = lax.psum_scatter(local_grads, "tile", scatter_dimension=0, tiled=True)
    share = lax.psum(share, "state")
    weight_grads = lax.all_gather(share, "tile", axis=0, tiled=True)
    return (county_mean[None, :], weight_grads)


def solution(mesh):
    in_specs = (
        P("state", None, "tile"),
        P("state", "tile"),
        P("state", "tile"),
        P("state", None),
        P("state", "tile"),
        P(),
        P(),
        P(),
        P(),
        P(),
    )
    out_specs = (P("state", "tile"), P())
    return jax.shard_map(
        on_device, mesh=mesh, in_specs=in_specs, out_specs=out_specs, check_vma=False
    )
```

profile of v0, /device:TPU:0, one launch (start us, length us, event | category | flops | bytes accessed | tf_op | source)
XLA Modules:
  0.0 223.0 jit_solution(9539927611696548798)
XLA Ops:
  7.2 0.8 slice_bitcast_fusion.5
  8.0 4.7 %fusion.5 = f32[64,128,128]{2,0,1:T(8,128)S(1)} fusion(bf16[64,240]{1,0:T(8,128)(2,1)} %param.15, bf16[1,240,16384]{2,1,0:T(8,128)(2,1)} %param.10), kind=kOutput, calls=%fused_computation.18 | convolution fusion | flops 503316480 | bytes 12089344 | tf_op jit(solution)/shard_map/dot_general | solution.py:59
  12.8 2.4 %fusion.18 = bf16[64,16384]{1,0:T(8,128)(2,1)S(1)} fusion(f32[64,128,128]{2,0,1:T(8,128)S(1)} %fusion.5, f32[64]{0:T(128)S(1)} %get-tuple-element.15, f32[64]{0:T(128)S(1)} %get-tuple-element.16, f32[64]{0:T(128)S(1)} %get-tuple-element.14), kind=kLoop, calls=%fused_computation.34 | loop fusion | flops 10485760 | bytes 6292224 | tf_op jit(solution)/shard_map/convert_element_type | solution.py:61
  15.2 4.6 %multiply_convert_fusion = (bf16[128,16384]{0,1:T(8,128)(2,1)S(1)}, f32[128,16384]{0,1:T(8,128)}) fusion(bf16[64,16384]{1,0:T(8,128)(2,1)S(1)} %fusion.18, bf16[128,64]{0,1:T(8,128)(2,1)S(1)} %copy-done.12), kind=kOutput, calls=%fused_computation.16 | convolution fusion | flops 278921216 | bytes 14696448 | tf_op jit(solution)/shard_map/dot_general | solution.py:62
  19.8 4.6 %add_convert_fusion = (bf16[128,16384]{0,1:T(8,128)(2,1)S(1)}, f32[128,16384]{0,1:T(8,128)}) fusion(bf16[128,16384]{0,1:T(8,128)(2,1)S(1)} %get-tuple-element.39, bf16[128,128]{1,0:T(8,128)(2,1)S(1)} %copy-done), kind=kOutput, calls=%fused_computation.14 | convolution fusion | flops 551550976 | bytes 16809984 | tf_op jit(solution)/shard_map/dot_general | solution.py:64
  24.5 1.9 copy-done.3
  26.5 1.2 fusion.38
  27.6 0.1 reduce_sum.147
  27.8 0.1 convert_reduce_fusion
  27.9 0.2 select_reduce_fusion.6
  28.1 0.2 convert_reduce_fusion.1
  28.5 0.5 collective-permute-start.3
  29.0 2.5 %collective-permute-start.4 = (f32[4]{0:T(128)S(1)}, f32[4]{0:T(128)S(1)}, u32[]{:S(2)}, u32[]{:S(2)}) collective-permute-start(f32[4]{0:T(128)S(1)} %get-tuple-element.27), channel_id=1, source_target_pairs={{0,2},{1,3},{2,4},{3,5},{4,6},{5,7},{6,0},{7,1},{8,10},{9,11},{10,... | collective-permute-start | bytes 56 | tf_op jit(solution)/shard_map/ppermute | solution.py:12
  31.5 2.4 %collective-permute-start.5 = (f32[4]{0:T(128)S(1)}, f32[4]{0:T(128)S(1)}, u32[]{:S(2)}, u32[]{:S(2)}) collective-permute-start(f32[4]{0:T(128)S(1)} %get-tuple-element.26), channel_id=1, source_target_pairs={{0,3},{1,4},{2,5},{3,6},{4,7},{5,0},{6,1},{7,2},{8,11},{9,12},{10,... | collective-permute-start | bytes 56 | tf_op jit(solution)/shard_map/ppermute | solution.py:12
  33.9 0.4 collective-permute-start.1
  34.4 2.5 %collective-permute-start.2 = (f32[4]{0:T(128)S(1)}, f32[4]{0:T(128)S(1)}, u32[]{:S(2)}, u32[]{:S(2)}) collective-permute-start(f32[4]{0:T(128)S(1)} %get-tuple-element.30), channel_id=1, source_target_pairs={{0,3},{1,4},{2,5},{3,6},{4,7},{5,0},{6,1},{7,2},{8,11},{9,12},{10,... | collective-permute-start | bytes 56 | tf_op jit(solution)/shard_map/ppermute | solution.py:12
  36.9 1.6 collective-permute-start.7
  38.6 1.3 collective-permute-start.8
  40.0 0.8 collective-permute-done.6
  40.8 0.6 collective-permute-done.7
  41.4 0.1 collective-permute-done.8
  41.8 0.5 fusion.40
  42.3 0.2 fusion.28
  42.6 2.3 %collective-permute-start.9 = (f32[4]{0:T(128)S(1)}, f32[4]{0:T(128)S(1)}, u32[]{:S(2)}, u32[]{:S(2)}) collective-permute-start(f32[4]{0:T(128)S(1)} %get-tuple-element.24), channel_id=1, source_target_pairs={{0,7},{1,0},{2,1},{3,2},{4,3},{5,4},{6,5},{7,6},{8,15},{9,8},{10,9... | collective-permute-start | bytes 56 | tf_op jit(solution)/shard_map/ppermute | solution.py:12
  44.8 1.4 collective-permute-start.10
  46.3 2.1 collective-permute-done.10
  48.4 0.9 collective-permute-done.11
  49.3 0.2 select_reduce_fusion.1
  49.7 10.0 %fusion.4 = bf16[128,16384]{0,1:T(8,128)(2,1)S(1)} fusion(f32[128,16384]{0,1:T(8,128)} %get-tuple-element.42, f32[16384]{0:T(1024)S(1)} %get-tuple-element.20, f32[128]{0:T(128)S(1)} %convert_element_type.84), kind=kLoop, calls=%fused_computation.13 | loop fusion | flops 20971520 | bytes 12648960 | tf_op jit(solution)/shard_map/convert_element_type | solution.py:75
  59.7 1.4 convolution_bitcast_fusion.4
  61.2 0.8 slice-done.1
  61.9 7.6 %fusion.2 = bf16[128,16384]{0,1:T(8,128)(2,1)S(1)} fusion(bf16[128,16384]{0,1:T(8,128)(2,1)S(1)} %fusion.4, bf16[128,128]{1,0:T(8,128)(2,1)S(1)} %copy-done, f32[128,16384]{0,1:T(8,128)S(1)} %bitcast.182, f32[16384]{0:T(1024)S(1)} %get-tuple-element.20, f32[128]{0:T(128)S(1)} %convert_element_type.84), kind=kOutput, calls=%fused_computation.5 | convolution fusion | flops 559939584 | bytes 16876032 | tf_op jit(solution)/shard_map/dot_general | solution.py:53
  69.5 3.5 %fusion.21 = f32[8,128,8,128]{3,2,1,0:T(8,128)S(1)} fusion(bf16[128,16384]{0,1:T(8,128)(2,1)S(1)} %fusion.2, bf16[128,64]{0,1:T(8,128)(2,1)S(1)} %copy-done.12, f32[64,128,128]{2,0,1:T(8,128)S(1)} %copy-done.2, f32[64]{0:T(128)S(1)} %get-tuple-element.15, f32[64]{0:T(128)S(1)} %get-tuple-element.16, f32[64]{0:T(128)S(1)} %get-tuple-element.14), kind=kOutput, calls=%fused_computation.43 | convolution fusion | flops 282066944 | bytes 12600064 | tf_op jit(solution)/shard_map/dot_general | solution.py:53
  73.0 2.5 %multiply_reduce_fusion.2 = (f32[64]{0:T(128)S(1)}, f32[64]{0:T(128)S(1)}, f32[64]{0:T(128)S(1)}) fusion(f32[64,128,128]{2,0,1:T(8,128)S(1)} %copy-done.2, f32[8,128,8,128]{3,2,1,0:T(8,128)S(1)} %fusion.21), kind=kLoop, calls=%fused_computation.40 | loop fusion | flops 6291264 | bytes 8389376 | tf_op jit(solution)/shard_map/reduce_sum | solution.py:39
  75.5 2.5 %copy.64 = f32[8,128,8,128]{3,2,0,1:T(8,128)} copy(f32[8,128,8,128]{3,2,1,0:T(8,128)S(1)} %fusion.21) | data formatting | bytes 8388608 | tf_op jit(solution)/shard_map/reshape | solution.py:22
  78.0 1.3 fusion.42
  79.3 0.8 copy-done.4
  80.2 0.7 convolution_bitcast_fusion.5
  80.9 9.3 %fusion.8 = f32[64,240]{1,0:T(8,128)S(1)} fusion(bf16[1,240,16384]{2,1,0:T(8,128)(2,1)} %param.10, f32[64,128,128]{2,0,1:T(8,128)} %bitcast.160, f32[64]{0:T(128)S(1)} %get-tuple-element.14, f32[64]{0:T(128)S(1)} %get-tuple-element.16, f32[64]{0:T(128)S(1)} %get-tuple-element.15), kind=kOutput, calls=%fused_computation.21 | convolution fusion | flops 509607936 | bytes 12120832 | tf_op jit(solution)/shard_map/dot_general | solution.py:47
  90.4 0.8 concatenate.3
  91.3 0.6 fusion.41
  93.2 50.4 %all-reduce.9.cloned.1.call-done = f32[40256]{0:T(1024)} async-done(((f32[40256]{0:T(1024)}), f32[40256]{0:T(1024)}) %all-reduce.9.cloned.1.call-update) | async-done | bytes 161040
  143.6 0.8 dynamic-slice.2
  144.4 18.9 %psum.7 = f32[5032]{0:T(1024)S(1)} all-reduce(f32[5032]{0:T(1024)S(1)} %dynamic-slice.2), channel_id=1, replica_groups=mesh['state'=4,'tile'=8] {'state'}, use_global_device_ids=true, to_apply=%region_17.18 | all-reduce | flops 5032 | bytes 40256 | tf_op jit(solution)/shard_map/psum | solution.py:190
  163.3 0.4 dynamic-update-slice
  163.8 0.7 copy-done.7
  164.5 50.2 %all-reduce.7.cloned.1.call-done = f32[40256]{0:T(1024)} async-done(((f32[40256]{0:T(1024)}), f32[40256]{0:T(1024)}) %all-reduce.7.cloned.1.call-update) | async-done | bytes 161040
  214.6 1.6 copy.68
  (72 shorter events, 1.6 us)
Async XLA Ops:
  7.2 12.7 %copy-start = (bf16[128,128]{1,0:T(8,128)(2,1)S(1)}, bf16[128,128]{1,0:T(8,128)(2,1)}, u32[]{:S(2)}) copy-start(bf16[128,128]{1,0:T(8,128)(2,1)} %param.18) | copy-start | bytes 98308
  7.2 136.4 %all-reduce.9.cloned.1.call-start = ((), (), s32[]{:S(2)}) async-start(), calls=%async_computation.1 | async-start | bytes 327680
  12.8 7.1 %copy-start.1 = (f32[64,128,128]{2,0,1:T(8,128)}, f32[64,128,128]{2,0,1:T(8,128)S(1)}, u32[]{:S(2)}) copy-start(f32[64,128,128]{2,0,1:T(8,128)S(1)} %fusion.5) | copy-start | bytes 12582916
  12.8 2.4 %copy-start.12 = (bf16[128,64]{0,1:T(8,128)(2,1)S(1)}, bf16[128,64]{0,1:T(8,128)(2,1)}, u32[]{:S(2)}) copy-start(bf16[128,64]{0,1:T(8,128)(2,1)} %param.17) | copy-start | bytes 49156
  19.8 4.6 %copy-start.5 = (bf16[128,16384]{0,1:T(8,128)(2,1)}, bf16[128,16384]{0,1:T(8,128)(2,1)S(1)}, u32[]{:S(2)}) copy-start(bf16[128,16384]{0,1:T(8,128)(2,1)S(1)} %get-tuple-element.39) | copy-start | bytes 12582916
  19.8 6.6 %copy-start.9 = (bf16[128]{0:T(256)(128)(2,1)S(1)}, bf16[128]{0:T(256)(128)(2,1)}, u32[]{:S(2)}) copy-start(bf16[128]{0:T(256)(128)(2,1)} %param.19) | copy-start | bytes 772
  24.5 2.0 copy-start.3
  24.5 3.3 %copy-start.11 = (s32[1,128]{1,0:T(1,128)S(1)}, s32[1,128]{1,0:T(1,128)}, u32[]{:S(2)}) copy-start(s32[1,128]{1,0:T(1,128)} %param.11) | copy-start | bytes 1540
  24.5 3.4 %copy-start.13 = (s32[1,96]{1,0:T(1,128)S(1)}, s32[1,96]{1,0:T(1,128)}, u32[]{:S(2)}) copy-start(s32[1,96]{1,0:T(1,128)} %param.13) | copy-start | bytes 1156
  24.5 3.4 %copy-start.14 = (s32[1,8]{1,0:T(1,128)S(1)}, s32[1,8]{1,0:T(1,128)}, u32[]{:S(2)}) copy-start(s32[1,8]{1,0:T(1,128)} %param.12) | copy-start | bytes 100
  24.5 17.3 %copy-start.10 = (s32[1,12]{1,0:T(1,128)S(1)}, s32[1,12]{1,0:T(1,128)}, u32[]{:S(2)}) copy-start(s32[1,12]{1,0:T(1,128)} %param.14) | copy-start | bytes 148
  28.5 5.9 %collective-permute-start.3 = (f32[4]{0:T(128)S(1)}, f32[4]{0:T(128)S(1)}, u32[]{:S(2)}, u32[]{:S(2)}) collective-permute-start(f32[4]{0:T(128)S(1)} %get-tuple-element.28), channel_id=1, source_target_pairs={{0,1},{1,2},{2,3},{3,4},{4,5},{5,6},{6,7},{7,0},{8,9},{9,10},{10,1... | collective-permute-start | bytes 56 | tf_op jit(solution)/shard_map/ppermute | solution.py:12
  29.0 8.0 %collective-permute-start.4 = (f32[4]{0:T(128)S(1)}, f32[4]{0:T(128)S(1)}, u32[]{:S(2)}, u32[]{:S(2)}) collective-permute-start(f32[4]{0:T(128)S(1)} %get-tuple-element.27), channel_id=1, source_target_pairs={{0,2},{1,3},{2,4},{3,5},{4,6},{5,7},{6,0},{7,1},{8,10},{9,11},{10,... | collective-permute-start | bytes 56 | tf_op jit(solution)/shard_map/ppermute | solution.py:12
  31.5 5.4 %collective-permute-start.5 = (f32[4]{0:T(128)S(1)}, f32[4]{0:T(128)S(1)}, u32[]{:S(2)}, u32[]{:S(2)}) collective-permute-start(f32[4]{0:T(128)S(1)} %get-tuple-element.26), channel_id=1, source_target_pairs={{0,3},{1,4},{2,5},{3,6},{4,7},{5,0},{6,1},{7,2},{8,11},{9,12},{10,... | collective-permute-start | bytes 56 | tf_op jit(solution)/shard_map/ppermute | solution.py:12
  33.9 4.7 %collective-permute-start = (f32[4]{0:T(128)S(1)}, f32[4]{0:T(128)S(1)}, u32[]{:S(2)}, u32[]{:S(2)}) collective-permute-start(f32[4]{0:T(128)S(1)} %get-tuple-element.32), channel_id=1, source_target_pairs={{0,1},{1,2},{2,3},{3,4},{4,5},{5,6},{6,7},{7,0},{8,9},{9,10},{10,1... | collective-permute-start | bytes 56 | tf_op jit(solution)/shard_map/ppermute | solution.py:12
  33.9 6.0 %collective-permute-start.1 = (f32[4]{0:T(128)S(1)}, f32[4]{0:T(128)S(1)}, u32[]{:S(2)}, u32[]{:S(2)}) collective-permute-start(f32[4]{0:T(128)S(1)} %get-tuple-element.31), channel_id=1, source_target_pairs={{0,2},{1,3},{2,4},{3,5},{4,6},{5,7},{6,0},{7,1},{8,10},{9,11},{10,... | collective-permute-start | bytes 56 | tf_op jit(solution)/shard_map/ppermute | solution.py:12
  34.4 5.5 %collective-permute-start.2 = (f32[4]{0:T(128)S(1)}, f32[4]{0:T(128)S(1)}, u32[]{:S(2)}, u32[]{:S(2)}) collective-permute-start(f32[4]{0:T(128)S(1)} %get-tuple-element.30), channel_id=1, source_target_pairs={{0,3},{1,4},{2,5},{3,6},{4,7},{5,0},{6,1},{7,2},{8,11},{9,12},{10,... | collective-permute-start | bytes 56 | tf_op jit(solution)/shard_map/ppermute | solution.py:12
  36.9 3.9 %collective-permute-start.6 = (f32[4]{0:T(128)S(1)}, f32[4]{0:T(128)S(1)}, u32[]{:S(2)}, u32[]{:S(2)}) collective-permute-start(f32[4]{0:T(128)S(1)} %get-tuple-element.36), channel_id=1, source_target_pairs={{0,1},{1,2},{2,3},{3,4},{4,5},{5,6},{6,7},{7,0},{8,9},{9,10},{10,1... | collective-permute-start | bytes 56 | tf_op jit(solution)/shard_map/ppermute | solution.py:12
  36.9 4.5 %collective-permute-start.7 = (f32[4]{0:T(128)S(1)}, f32[4]{0:T(128)S(1)}, u32[]{:S(2)}, u32[]{:S(2)}) collective-permute-start(f32[4]{0:T(128)S(1)} %get-tuple-element.35), channel_id=1, source_target_pairs={{0,2},{1,3},{2,4},{3,5},{4,6},{5,7},{6,0},{7,1},{8,10},{9,11},{10,... | collective-permute-start | bytes 56 | tf_op jit(solution)/shard_map/ppermute | solution.py:12
  38.6 3.0 %collective-permute-start.8 = (f32[4]{0:T(128)S(1)}, f32[4]{0:T(128)S(1)}, u32[]{:S(2)}, u32[]{:S(2)}) collective-permute-start(f32[4]{0:T(128)S(1)} %get-tuple-element.34), channel_id=1, source_target_pairs={{0,3},{1,4},{2,5},{3,6},{4,7},{5,0},{6,1},{7,2},{8,11},{9,12},{10,... | collective-permute-start | bytes 56 | tf_op jit(solution)/shard_map/ppermute | solution.py:12
  42.6 3.7 %collective-permute-start.9 = (f32[4]{0:T(128)S(1)}, f32[4]{0:T(128)S(1)}, u32[]{:S(2)}, u32[]{:S(2)}) collective-permute-start(f32[4]{0:T(128)S(1)} %get-tuple-element.24), channel_id=1, source_target_pairs={{0,7},{1,0},{2,1},{3,2},{4,3},{5,4},{6,5},{7,6},{8,15},{9,8},{10,9... | collective-permute-start | bytes 56 | tf_op jit(solution)/shard_map/ppermute | solution.py:12
  44.8 3.5 %collective-permute-start.10 = (f32[4]{0:T(128)S(1)}, f32[4]{0:T(128)S(1)}, u32[]{:S(2)}, u32[]{:S(2)}) collective-permute-start(f32[4]{0:T(128)S(1)} %get-tuple-element.23), channel_id=1, source_target_pairs={{0,6},{1,7},{2,0},{3,1},{4,2},{5,3},{6,4},{7,5},{8,14},{9,15},{10,... | collective-permute-start | bytes 56 | tf_op jit(solution)/shard_map/ppermute | solution.py:12
  46.3 3.0 %collective-permute-start.11 = (f32[4]{0:T(128)S(1)}, f32[4]{0:T(128)S(1)}, u32[]{:S(2)}, u32[]{:S(2)}) collective-permute-start(f32[4]{0:T(128)S(1)} %get-tuple-element.22), channel_id=1, source_target_pairs={{0,5},{1,6},{2,7},{3,0},{4,1},{5,2},{6,3},{7,4},{8,13},{9,14},{10,... | collective-permute-start | bytes 56 | tf_op jit(solution)/shard_map/ppermute | solution.py:12
  49.7 10.0 %copy-start.6 = (bf16[128,16384]{0,1:T(8,128)(2,1)S(1)}, bf16[128,16384]{0,1:T(8,128)(2,1)}, u32[]{:S(2)}) copy-start(bf16[128,16384]{0,1:T(8,128)(2,1)} %copy-done.5) | copy-start | bytes 12582916
  49.7 11.4 %slice-start = ((s8[8388608]{0:T(1024)(128)(4,1)}), s8[4194304]{0:T(1024)(128)(4,1)S(1)}, s32[]{:S(2)}) async-start(s8[8388608]{0:T(1024)(128)(4,1)} %bitcast.181), calls=%async_computation.2 | async-start | bytes 8388608
  59.7 2.2 slice-start.1
  61.9 7.6 %copy-start.2 = (f32[64,128,128]{2,0,1:T(8,128)S(1)}, f32[64,128,128]{2,0,1:T(8,128)}, u32[]{:S(2)}) copy-start(f32[64,128,128]{2,0,1:T(8,128)} %copy-done.1) | copy-start | bytes 12582916
  78.0 2.2 copy-start.4
  80.9 10.3 %copy-start.8 = (u32[32]{0:T(128)S(1)}, u32[32]{0:T(128)}, u32[]{:S(2)}) copy-start(u32[32]{0:T(128)} %constant.78) | copy-start | bytes 388
  91.2 123.4 %all-reduce.7.cloned.1.call-start = ((), (), s32[]{:S(2)}) async-start(), calls=%async_computation | async-start | bytes 327680
  163.8 0.7 copy-start.7
Sparse Core Ops, SparseCore 0:
  91.3 52.2 all-reduce.8
  164.6 49.9 all-reduce.6
where the time goes:
time: 224 us; the launch traced here: 223 us
  waiting for transfers between devices  105 us (47%)
  matrix products  38.8 us (17%)
  blocking collectives  18.9 us (8%)
  other arithmetic  16.9 us (8%)
  between operations  15.6 us (7%)
  starting transfers between devices  15 us (7%)
  local copies, waits for them, and re-layouts  12.8 us (6%)
    unnamed x4, waiting for transfers between devices  101 us
    psum x1, blocking collectives, on_device(): share = lax.psum(share, 'state')  18.9 us
    ppermute x12, starting transfers between devices, from_behind(): lax.ppermute(value, axis, [(i, (i + by) % peers) for i in range(peers)])  14.9 us
    dot_general x3, matrix products, contract_last(): lax.dot_general(left, right, (((1,), (1,)), ((), ())), preferred_element_...  12 us
    dot_general x2, matrix products, contract_first(): lax.dot_general(left, right, (((0,), (0,)), ((), ())), preferred_element_...  11 us
    convert_element_type x1, other arithmetic, backward(): d_h3 = (d_a3 * silu_parts(h_three)[1]).astype(jnp.bfloat16)  9.98 us
    unnamed x39, local copies, waits for them, and re-layouts  7.74 us
    dot_general x1, matrix products, forward(): h_one = jnp.dot(w_first, pixels, preferred_element_type=jnp.float32)  4.75 us
  transfers between devices with their start and end apart: 14, of which 7 were waited for; matrix products, arithmetic and copies ran while one was open for 0% of the time, Pallas kernels for 0%

commit v1 on v0

v1 whole, which is shorter than its diff:
```python
import functools

import jax
import jax.numpy as jnp
from jax import lax
from jax.experimental import pallas as pl
from jax.experimental.pallas import tpu as pltpu
from jax.sharding import PartitionSpec as P

REACH = 4
LANES = 128
GROUP = 8
STEP_ROWS = 4
DMA_STEPS = 8
MESH = pl.DeviceIdType.MESH
F32 = jnp.float32
BF16 = jnp.bfloat16


def mm(left, right):
    return jnp.dot(left, right, preferred_element_type=F32)


def mm_last(left, right):
    return lax.dot_general(left, right, (((1,), (1,)), ((), ())), preferred_element_type=F32)


def iota(shape, dim):
    return lax.broadcasted_iota(jnp.int32, shape, dim)


def to_column(row, size):
    eye = iota((size, size), 0) == iota((size, size), 1)
    return jnp.sum(jnp.where(eye, row, 0.0), axis=1, keepdims=True)


def to_row(column, size):
    eye = iota((size, size), 0) == iota((size, size), 1)
    return jnp.sum(jnp.where(eye, column, 0.0), axis=0, keepdims=True)


def gate_parts(half):
    twice = jnp.tanh(half) + 1.0
    act = half * twice
    return act, twice + act * (2.0 - twice)


def kernel(
    n_tile, n_state, share,
    bands, slot_row, counties, table, label, w_first, taps, w_second, w_third, w_head,
    mean_out, grads_out,
    x_s, a1_s, a2_s, d1_s, d2_s, d3_s, slot_s, g_s, w2_s, w2t_s, w3_s, w3t_s, wh_s,
    acc_first, acc_second, acc_third, acc_head, first_lo, first_hi, second_s, third_s,
    flat, msg, msgs, parts, zparts, whole,
    x_sem, msg_send, msg_recv, part_send, part_recv, z_send, z_recv, all_send, all_recv,
):
    me = lax.axis_index("tile")
    my_state = lax.axis_index("state")
    c1, feat = w_first.shape
    c2 = w_second.shape[0]
    blocks = slot_row.shape[1]
    pixels = bands.shape[2]
    row_len = pixels // blocks
    cty_dev = label.shape[1]
    places = table.shape[1]
    slot_count = counties.shape[1]
    step_px = STEP_ROWS * row_len
    dma_px = pixels // DMA_STEPS
    steps_per_dma = dma_px // step_px

    def band_copy(k):
        cols = pl.ds(pl.multiple_of(k * dma_px, dma_px), dma_px)
        return pltpu.make_async_copy(bands.at[0, :, cols], x_s.at[:, cols], x_sem.at[k])

    for k in range(DMA_STEPS):
        band_copy(k).start()

    def tile_peer(by):
        return lax.rem(me + by + n_tile, n_tile)

    def state_peer(by):
        return lax.rem(my_state + by + n_state, n_state)

    barrier = pltpu.get_barrier_semaphore()
    for by in range(1, n_tile):
        pl.semaphore_signal(barrier, inc=1, device_id={"tile": tile_peer(by)}, device_id_type=MESH)
    for by in range(1, n_state):
        pl.semaphore_signal(
            barrier, inc=1, device_id={"state": state_peer(by)}, device_id_type=MESH
        )

    slots = slot_row[...].astype(F32)
    slot_s[...] = jnp.broadcast_to(to_column(slots, blocks), (blocks, LANES))
    half_second = w_second[...].astype(F32) * 0.5
    half_third = w_third[...].astype(F32) * 0.5
    w2_s[...] = half_second.astype(BF16)
    w3_s[...] = half_third.astype(BF16)
    w2t_s[...] = half_second.T.astype(BF16)
    w3t_s[...] = half_third.T.astype(BF16)
    head_row = w_head[...].astype(F32)
    wh_s[...] = jnp.broadcast_to(to_column(head_row, c2) * 0.5, (c2, LANES))
    tap_cols = [to_column(taps[k : k + 1, :], c1) for k in range(3)]
    lane = iota((c1, LANES), 1)
    tap_prev = jnp.where(lane == 0, 0.0, tap_cols[0] * 0.5)
    tap_here = jnp.broadcast_to(tap_cols[1] * 0.5, (c1, LANES))
    tap_next = jnp.where(lane == LANES - 1, 0.0, tap_cols[2] * 0.5)
    acc_first[...] = jnp.zeros_like(acc_first)
    acc_second[...] = jnp.zeros_like(acc_second)
    acc_third[...] = jnp.zeros_like(acc_third)
    acc_head[...] = jnp.zeros_like(acc_head)
    slot_ids = iota((2 * GROUP, LANES), 0).astype(F32)

    def row_cols(j):
        return slice(j * row_len, (j + 1) * row_len)

    def forward(step):
        cols = pl.ds(pl.multiple_of(step * step_px, step_px), step_px)
        h1 = mm(w_first[...], x_s[:, cols])
        s1 = []
        for j in range(STEP_ROWS):
            h = h1[:, row_cols(j)]
            s1.append(
                tap_prev * pltpu.roll(h, 1, 1)
                + tap_here * h
                + tap_next * pltpu.roll(h, LANES - 1, 1)
            )
        a1, d1 = gate_parts(jnp.concatenate(s1, axis=1))
        d1_s[:, cols] = d1
        a1 = a1.astype(BF16)
        a1_s[:, cols] = a1
        a2, d2 = gate_parts(mm(w2_s[...], a1))
        d2_s[:, cols] = d2
        a2 = a2.astype(BF16)
        a2_s[:, cols] = a2
        a3, d3 = gate_parts(mm(w3_s[...], a2))
        d3_s[:, cols] = d3
        a3 = (a3 + a2.astype(F32)).astype(BF16)
        member = jnp.concatenate(
            [
                (slot_s[pl.ds(step * STEP_ROWS + j, 1), :] == slot_ids).astype(F32)
                for j in range(STEP_ROWS)
            ],
            axis=1,
        ).astype(BF16)
        acc_head[...] += mm_last(member, a3)

    def forward_dma(k, carry):
        band_copy(k).wait()

        def inner(i, c):
            forward(k * steps_per_dma + i)
            return c

        return lax.fori_loop(0, steps_per_dma, inner, carry)

    lax.fori_loop(0, DMA_STEPS, forward_dma, 0)

    head_sums = acc_head[0:GROUP, :]
    slot_sums = jnp.sum(head_sums * head_row, axis=1, keepdims=True)
    in_slot = (slots == slot_ids[0:GROUP, :]).astype(F32)
    slot_counts = jnp.sum(in_slot, axis=1, keepdims=True) * float(row_len)
    county = to_column(counties[...].astype(F32), slot_count)
    hits = county == iota((slot_count, places), 1).astype(F32)
    place = jnp.sum(jnp.where(hits, table[...].astype(F32), 0.0), axis=1, keepdims=True)
    place = place - (me * cty_dev).astype(F32)
    place = jnp.where(place < 0.0, place + float(places), place)
    pick = (place == iota((slot_count, LANES), 1).astype(F32)).astype(F32)
    msg[...] = jnp.zeros_like(msg)
    msg[0:1, :] = jnp.sum(pick * slot_sums, axis=0, keepdims=True)
    msg[1:2, :] = jnp.sum(pick * slot_counts, axis=0, keepdims=True)
    msg[2:3, 0:cty_dev] = label[...].astype(F32)

    pl.semaphore_wait(barrier, n_tile - 1 + n_state - 1)
    offsets = [by for by in range(1 - REACH, REACH) if by]
    copies = []
    for n, by in enumerate(offsets):
        copies.append(
            pltpu.make_async_remote_copy(
                src_ref=msg,
                dst_ref=msgs.at[n],
                send_sem=msg_send.at[n],
                recv_sem=msg_recv.at[n],
                device_id={"tile": tile_peer(by)},
                device_id_type=MESH,
            )
        )
        copies[-1].start()
    total = msg[...]
    for n, by in enumerate(offsets):
        copies[n].wait_recv()
        total = total + pltpu.roll(msgs[n], (-by * cty_dev) % LANES, 1)
    for copy in copies:
        copy.wait_send()
    sums, counts, target = total[0:1, :], total[1:2, :], total[2:3, :] * 0.01
    denom = jnp.maximum(counts, 1.0)
    mean = sums / denom
    mean_out[...] = mean[:, 0:cty_dev]
    adjoint = jnp.where(
        counts > 0.5, 2.0 * (mean - target) / (float(n_tile * n_state) * denom), 0.0
    )
    slot_g = jnp.sum(jnp.where(pick > 0.5, adjoint, 0.0), axis=1, keepdims=True)
    slot_g = slot_g.astype(BF16).astype(F32)
    all_slots = slot_s[...]
    g_rows = jnp.zeros((blocks, LANES), F32)
    for s in range(slot_count):
        g_rows = jnp.where(all_slots == float(s), slot_g[s : s + 1, 0:1], g_rows)
    g_s[...] = g_rows

    def backward(step, carry):
        cols = pl.ds(pl.multiple_of(step * step_px, step_px), step_px)
        x = x_s[:, cols]
        a1 = a1_s[:, cols]
        a2 = a2_s[:, cols]
        wh = wh_s[...]
        d_a3 = jnp.concatenate(
            [wh * g_s[pl.ds(step * STEP_ROWS + j, 1), :] for j in range(STEP_ROWS)], axis=1
        )
        d_h3 = (d_a3 * d3_s[:, cols]).astype(BF16)
        acc_third[...] += mm_last(d_h3, a2)
        d_h2 = ((mm(w3t_s[...], d_h3) + d_a3) * d2_s[:, cols]).astype(BF16)
        acc_second[...] += mm_last(d_h2, a1)
        d_s1 = mm(w2t_s[...], d_h2) * d1_s[:, cols]
        left, right = [], []
        for j in range(STEP_ROWS):
            d = d_s1[:, row_cols(j)]
            left.append(jnp.where(lane == LANES - 1, 0.0, pltpu.roll(d, LANES - 1, 1)))
            right.append(jnp.where(lane == 0, 0.0, pltpu.roll(d, 1, 1)))
        shifted = jnp.concatenate(
            [jnp.concatenate(left, axis=1), d_s1, jnp.concatenate(right, axis=1)], axis=0
        ).astype(BF16)
        acc_first[...] += mm_last(shifted, x)
        return carry

    lax.fori_loop(0, pixels // step_px, backward, 0)

    g_first = [acc_first[k * c1 : (k + 1) * c1, :] for k in range(3)]
    weights = w_first[...].astype(F32)
    d_first = tap_cols[0] * g_first[0] + tap_cols[1] * g_first[1] + tap_cols[2] * g_first[2]
    tap_rows = [
        to_row(jnp.sum(weights * g, axis=1, keepdims=True), c1) for g in g_first
    ]
    d_head = jnp.sum(head_sums * slot_g, axis=0, keepdims=True)
    first_lo[...] = d_first[:, 0:LANES]
    first_hi[:, 0 : feat - LANES] = d_first[:, LANES:feat]
    flat[...] = jnp.zeros_like(flat)
    period = feat * GROUP // LANES
    groups = c1 // GROUP
    at = iota((groups, LANES), 1)
    for j in range(period):
        chan, off = divmod(j * LANES, feat)
        lo = first_lo[pl.ds(chan, groups, stride=GROUP), :]
        hi = first_hi[pl.ds(chan, groups, stride=GROUP), :]
        value = pltpu.roll(hi, (-off) % LANES, 1)
        if off < LANES:
            lo_part = pltpu.roll(lo, (-off) % LANES, 1) if off else lo
            value = jnp.where(at < LANES - off, lo_part, value)
        if off + LANES > feat:
            after = first_lo[pl.ds(chan + 1, groups, stride=GROUP), :]
            value = jnp.where(at < feat - off, value, pltpu.roll(after, (feat - off) % LANES, 1))
        flat[pl.ds(j, groups, stride=period), :] = value
    base = c1 * feat // LANES
    half = LANES // 2
    second_s[...] = jnp.zeros_like(second_s)
    second_s[0:c2, 0:half] = acc_second[...]
    third_s[0:c2, :] = acc_third[...]
    third_s[c2 : c2 + 1, :] = d_head
    second_s[c2 : c2 + 1, :] = third_s[0:1, :]
    one = iota((1, LANES), 1) < half
    flat[base : base + 1, :] = jnp.concatenate(tap_rows[0:2], axis=1)
    flat[base + 1 : base + 2, :] = jnp.where(
        one,
        jnp.concatenate([tap_rows[2], tap_rows[2]], axis=1),
        pltpu.roll(second_s[0:1, :], half, 1),
    )
    odd = second_s[pl.ds(1, c2 // 2, stride=2), :]
    even = second_s[pl.ds(2, c2 // 2, stride=2), :]
    low = iota((c2 // 2, LANES), 1) < half
    flat[base + 2 : base + 2 + c2 // 2, :] = jnp.where(low, odd, pltpu.roll(even, half, 1))
    start = base + 2 + c2 // 2
    low = iota((c2, LANES), 1) < half
    flat[start : start + c2, :] = jnp.where(
        low, pltpu.roll(third_s[0:c2, :], half, 1), pltpu.roll(third_s[1 : c2 + 1, :], half, 1)
    )
    flat[start + c2 : start + c2 + 1, :] = jnp.where(one, pltpu.roll(d_head, half, 1), 0.0)

    def share_of(index):
        return pl.ds(pl.multiple_of(index * share, share), share)

    copies = []
    for by in range(1, n_tile):
        peer = tile_peer(by)
        copies.append(
            pltpu.make_async_remote_copy(
                src_ref=flat.at[share_of(peer)],
                dst_ref=parts.at[by - 1],
                send_sem=part_send.at[by - 1],
                recv_sem=part_recv.at[by - 1],
                device_id={"tile": peer},
                device_id_type=MESH,
            )
        )
        copies[-1].start()
    piece = flat[share_of(me), :]
    for n, copy in enumerate(copies):
        copy.wait_recv()
        piece = piece + parts[n]
    zparts[my_state] = piece
    zcopies = []
    for by in range(1, n_state):
        zcopies.append(
            pltpu.make_async_remote_copy(
                src_ref=zparts.at[my_state],
                dst_ref=zparts.at[my_state],
                send_sem=z_send.at[by - 1],
                recv_sem=z_recv.at[by - 1],
                device_id={"state": state_peer(by)},
                device_id_type=MESH,
            )
        )
        zcopies[-1].start()
    for copy in zcopies:
        copy.wait_recv()
    piece = zparts[0]
    for s in range(1, n_state):
        piece = piece + zparts[s]
    whole[share_of(me), :] = piece
    acopies = []
    for by in range(1, n_tile):
        acopies.append(
            pltpu.make_async_remote_copy(
                src_ref=whole.at[share_of(me)],
                dst_ref=whole.at[share_of(me)],
                send_sem=all_send.at[by - 1],
                recv_sem=all_recv.at[by - 1],
                device_id={"tile": tile_peer(by)},
                device_id_type=MESH,
            )
        )
        acopies[-1].start()
    for copy in copies:
        copy.wait_send()
    for copy in zcopies:
        copy.wait_send()
    for copy in acopies:
        copy.wait_recv()
    for copy in acopies:
        copy.wait_send()
    grads_out[...] = whole[...]


def on_device(
    n_tile, n_state,
    bands, block_slot, tile_counties, county_place, label, w_first, taps, w_second, w_third, w_head,
):
    feat, pixels = bands.shape[1:]
    c1, c2 = w_first.shape[0], w_second.shape[0]
    blocks = block_slot.shape[1]
    grads = c1 * feat + 3 * c1 + c2 * c1 + c2 * c2 + c2
    rows = pl.cdiv(grads, LANES)
    share = pl.cdiv(rows, n_tile * GROUP) * GROUP
    vmem = pl.BlockSpec(memory_space=pltpu.VMEM)
    dma = pltpu.SemaphoreType.DMA
    near = 2 * (REACH - 1)
    mean, out = pl.pallas_call(
        functools.partial(kernel, n_tile, n_state, share),
        out_shape=(
            jax.ShapeDtypeStruct(label.shape, F32),
            jax.ShapeDtypeStruct((n_tile * share, LANES), F32),
        ),
        in_specs=[pl.BlockSpec(memory_space=pl.ANY)] + [vmem] * 9,
        out_specs=(vmem, vmem),
        scratch_shapes=[
            pltpu.VMEM((feat, pixels), BF16),
            pltpu.VMEM((c1, pixels), BF16),
            pltpu.VMEM((c2, pixels), BF16),
            pltpu.VMEM((c1, pixels), F32),
            pltpu.VMEM((c2, pixels), F32),
            pltpu.VMEM((c2, pixels), F32),
            pltpu.VMEM((blocks, LANES), F32),
            pltpu.VMEM((blocks, LANES), F32),
            pltpu.VMEM((c2, c1), BF16),
            pltpu.VMEM((c1, c2), BF16),
            pltpu.VMEM((c2, c2), BF16),
            pltpu.VMEM((c2, c2), BF16),
            pltpu.VMEM((c2, LANES), F32),
            pltpu.VMEM((3 * c1, feat), F32),
            pltpu.VMEM((c2, c1), F32),
            pltpu.VMEM((c2, c2), F32),
            pltpu.VMEM((2 * GROUP, c2), F32),
            pltpu.VMEM((c1, LANES), F32),
            pltpu.VMEM((c1, LANES), F32),
            pltpu.VMEM((c2 + GROUP, LANES), F32),
            pltpu.VMEM((c2 + GROUP, LANES), F32),
            pltpu.VMEM((n_tile * share, LANES), F32),
            pltpu.VMEM((GROUP, LANES), F32),
            pltpu.VMEM((near, GROUP, LANES), F32),
            pltpu.VMEM((n_tile - 1, share, LANES), F32),
            pltpu.VMEM((n_state, share, LANES), F32),
            pltpu.VMEM((n_tile * share, LANES), F32),
            dma((DMA_STEPS,)),
            dma((near,)),
            dma((near,)),
            dma((n_tile - 1,)),
            dma((n_tile - 1,)),
            dma((n_state - 1,)),
            dma((n_state - 1,)),
            dma((n_tile - 1,)),
            dma((n_tile - 1,)),
        ],
        compiler_params=pltpu.CompilerParams(
            collective_id=0, has_side_effects=True, vmem_limit_bytes=56 * 2**20
        ),
    )(
        bands, block_slot, tile_counties, county_place, label,
        w_first, taps, w_second, w_third, w_head.reshape(1, -1),
    )
    return mean, out.reshape(-1)[:grads]


def solution(mesh):
    in_specs = (
        P("state", None, "tile"),
        P("state", "tile"),
        P("state", "tile"),
        P("state", None),
        P("state", "tile"),
        P(),
        P(),
        P(),
        P(),
        P(),
    )
    return jax.shard_map(
        functools.partial(on_device, mesh.shape["tile"], mesh.shape["state"]),
        mesh=mesh,
        in_specs=in_specs,
        out_specs=(P("state", "tile"), P()),
        check_vma=False,
    )
```

time: 224 us -> 74 us (0.33)
  waiting for transfers between devices: 105 us -> 0 us
  Pallas kernels: 0 us -> 68.9 us
  matrix products: 38.8 us -> 0 us
  blocking collectives: 18.9 us -> 0 us
  other arithmetic: 16.9 us -> 0 us
  starting transfers between devices: 15 us -> 0 us
  between operations: 15.6 us -> 0.64 us
  local copies, waits for them, and re-layouts: 12.8 us -> 4.16 us
    unnamed x4 -> x0, waiting for transfers between devices: 101 us -> none
    pallas_call x0 -> x1, Pallas kernels: none -> 68.9 us  [on_device(): pl.pallas_call(functools.partial(kernel, n_tile, n_state, share), out_sha...]
    dot_general x10 -> x0, matrix products: 38.8 us -> none  [the longest x3 12 us: contract_last(): lax.dot_general(left, right, (((1,), (1,)), ((), ())), preferred_element_...]
    psum x1 -> x0, blocking collectives: 18.9 us -> none  [on_device(): share = lax.psum(share, 'state')]
    ppermute x12 -> x0, starting transfers between devices: 14.9 us -> none  [from_behind(): lax.ppermute(value, axis, [(i, (i + by) % peers) for i in range(peers)])]
    convert_element_type x6 -> x0, other arithmetic: 12.5 us -> none  [the longest x1 9.98 us: backward(): d_h3 = (d_a3 * silu_parts(h_three)[1]).astype(jnp.bfloat16)]
    ppermute x12 -> x0, waiting for transfers between devices: 4.51 us -> none  [from_behind(): lax.ppermute(value, axis, [(i, (i + by) % peers) for i in range(peers)])]
    reduce_sum x10 -> x0, other arithmetic: 3.74 us -> none  [the longest x1 2.48 us: tap_grads(): jnp.sum(above * padded[:, :, :-2], axis=(1, 2))]
  transfers between devices with their start and end apart: 14 -> 0, of which waited for: 7 -> 0; matrix products, arithmetic and copies ran while one was open for 0% -> 0% of each run, Pallas kernels for 0% -> 0%
where the time goes in v1:
time: 74 us; the launch traced here: 73.7 us
  Pallas kernels  68.9 us (93%)
  local copies, waits for them, and re-layouts  4.16 us (6%)
    pallas_call x1, Pallas kernels, on_device(): pl.pallas_call(functools.partial(kernel, n_tile, n_state, share), out_sha...  68.9 us
    unnamed x3, local copies, waits for them, and re-layouts  4.16 us

profile of v1, /device:TPU:0, one launch (start us, length us, event | category | flops | bytes accessed | tf_op | source)
XLA Modules:
  0.0 73.7 jit_solution(15961795073730728553)
XLA Ops:
  0.6 1.4 %copy.12.w_second = bf16[128,64]{1,0:T(8,128)(2,1)} copy(bf16[128,64]{0,1:T(8,128)(2,1)} %param.17) | data formatting | bytes 32768 | tf_op args[7]
  2.1 68.9 %shard_map.113 = (f32[1,12]{1,0:T(1,128)}, f32[320,128]{1,0:T(8,128)}) custom-call(bf16[1,240,16384]{2,1,0:T(8,128)(2,1)} %bands.1, s32[1,128]{1,0:T(1,128)} %slot_row.1, s32[1,8]{1,0:T(1,128)} %counties.1, s32[1,96]{1,0:T(1,128)} %table.1, s32[1,12]{1,0:T(1,128)} %label.1, bf16[64,240]{1,0:T(8,128)(2,1)} %w_first.1, f32[3,64]{1,0:T(4,128)} %taps.1, ...), custom_call_target="tpu_custom_call" | custom-call | tf_op jit(solution)/shard_map/pallas_call | solution.py:364
  71.0 1.1 %copy.15 = f32[1,12]{1,0:T(1,128)} copy(f32[1,12]{1,0:T(1,128)} %get-tuple-element.8) | data formatting | bytes 96
  72.1 1.6 %copy.16 = f32[40256]{0:T(1024)} copy(f32[40256]{0:T(1024)} %bitcast.3) | data formatting | bytes 322048

commit v2 on v1

--- a/solution.py
+++ b/solution.py
@@ -10,7 +10,7 @@
 REACH = 4
 LANES = 128
 GROUP = 8
-STEP_ROWS = 4
+STEP_ROWS = 8
 DMA_STEPS = 8
 MESH = pl.DeviceIdType.MESH
 F32 = jnp.float32
@@ -57,7 +57,7 @@
     me = lax.axis_index("tile")
     my_state = lax.axis_index("state")
     c1, feat = w_first.shape
-    c2 = w_second.shape[0]
+    c2 = w_second.shape[1]
     blocks = slot_row.shape[1]
     pixels = bands.shape[2]
     row_len = pixels // blocks
@@ -93,9 +93,9 @@
     slot_s[...] = jnp.broadcast_to(to_column(slots, blocks), (blocks, LANES))
     half_second = w_second[...].astype(F32) * 0.5
     half_third = w_third[...].astype(F32) * 0.5
-    w2_s[...] = half_second.astype(BF16)
+    w2t_s[...] = half_second.astype(BF16)
     w3_s[...] = half_third.astype(BF16)
-    w2t_s[...] = half_second.T.astype(BF16)
+    w2_s[...] = half_second.T.astype(BF16)
     w3t_s[...] = half_third.T.astype(BF16)
     head_row = w_head[...].astype(F32)
     wh_s[...] = jnp.broadcast_to(to_column(head_row, c2) * 0.5, (c2, LANES))
@@ -412,7 +412,7 @@
         ),
     )(
         bands, block_slot, tile_counties, county_place, label,
-        w_first, taps, w_second, w_third, w_head.reshape(1, -1),
+        w_first, taps, w_second.T, w_third, w_head.reshape(1, -1),
     )
     return mean, out.reshape(-1)[:grads]
 

time: 74 us -> 53.4 us (0.72)
  Pallas kernels: 68.9 us -> 49.8 us
  local copies, waits for them, and re-layouts: 4.16 us -> 2.73 us
    pallas_call x1, Pallas kernels: 68.9 us -> 49.8 us  [on_device(): pl.pallas_call(functools.partial(kernel, n_tile, n_state, share), out_sha...]
    unnamed x3 -> x2, local copies, waits for them, and re-layouts: 4.16 us -> 2.73 us
where the time goes in v2:
time: 53.4 us; the launch traced here: 53.2 us
  Pallas kernels  49.8 us (93%)
  local copies, waits for them, and re-layouts  2.73 us (5%)
  between operations  0.64 us (1%)
    pallas_call x1, Pallas kernels, on_device(): pl.pallas_call(functools.partial(kernel, n_tile, n_state, share), out_sha...  49.8 us
    unnamed x2, local copies, waits for them, and re-layouts  2.73 us

profile of v2, /device:TPU:0, one launch (start us, length us, event | category | flops | bytes accessed | tf_op | source)
XLA Modules:
  0.0 53.2 jit_solution(5552950198749813570)
XLA Ops:
  0.6 49.8 %shard_map.113 = (f32[1,12]{1,0:T(1,128)}, f32[320,128]{1,0:T(8,128)}) custom-call(bf16[1,240,16384]{2,1,0:T(8,128)(2,1)} %bands.1, s32[1,128]{1,0:T(1,128)} %slot_row.1, s32[1,8]{1,0:T(1,128)} %counties.1, s32[1,96]{1,0:T(1,128)} %table.1, s32[1,12]{1,0:T(1,128)} %label.1, bf16[64,240]{1,0:T(8,128)(2,1)} %w_first.1, f32[3,64]{1,0:T(4,128)} %taps.1, ...), custom_call_target="tpu_custom_call" | custom-call | tf_op jit(solution)/shard_map/pallas_call | solution.py:364
  50.5 1.1 %copy.14 = f32[1,12]{1,0:T(1,128)} copy(f32[1,12]{1,0:T(1,128)} %get-tuple-element.8) | data formatting | bytes 96
  51.6 1.6 %copy.15 = f32[40256]{0:T(1024)} copy(f32[40256]{0:T(1024)} %bitcast.4) | data formatting | bytes 322048

commit v3 on v2

--- a/solution.py
+++ b/solution.py
@@ -10,7 +10,7 @@
 REACH = 4
 LANES = 128
 GROUP = 8
-STEP_ROWS = 8
+STEP_ROWS = 16
 DMA_STEPS = 8
 MESH = pl.DeviceIdType.MESH
 F32 = jnp.float32

time: 53.4 us -> 45.3 us (0.85)
  Pallas kernels: 49.8 us -> 41.7 us
    pallas_call x1, Pallas kernels: 49.8 us -> 41.7 us  [on_device(): pl.pallas_call(functools.partial(kernel, n_tile, n_state, share), out_sha...]
where the time goes in v3:
time: 45.3 us; the launch traced here: 45 us
  Pallas kernels  41.7 us (92%)
  local copies, waits for them, and re-layouts  2.73 us (6%)
  between operations  0.64 us (1%)
    pallas_call x1, Pallas kernels, on_device(): pl.pallas_call(functools.partial(kernel, n_tile, n_state, share), out_sha...  41.7 us
    unnamed x2, local copies, waits for them, and re-layouts  2.73 us

profile of v3, /device:TPU:0, one launch (start us, length us, event | category | flops | bytes accessed | tf_op | source)
XLA Modules:
  0.0 45.0 jit_solution(2073782533977840722)
XLA Ops:
  0.6 41.7 %shard_map.113 = (f32[1,12]{1,0:T(1,128)}, f32[320,128]{1,0:T(8,128)}) custom-call(bf16[1,240,16384]{2,1,0:T(8,128)(2,1)} %bands.1, s32[1,128]{1,0:T(1,128)} %slot_row.1, s32[1,8]{1,0:T(1,128)} %counties.1, s32[1,96]{1,0:T(1,128)} %table.1, s32[1,12]{1,0:T(1,128)} %label.1, bf16[64,240]{1,0:T(8,128)(2,1)} %w_first.1, f32[3,64]{1,0:T(4,128)} %taps.1, ...), custom_call_target="tpu_custom_call" | custom-call | tf_op jit(solution)/shard_map/pallas_call | solution.py:364
  42.3 1.1 %copy.14 = f32[1,12]{1,0:T(1,128)} copy(f32[1,12]{1,0:T(1,128)} %get-tuple-element.8) | data formatting | bytes 96
  43.5 1.6 %copy.15 = f32[40256]{0:T(1024)} copy(f32[40256]{0:T(1024)} %bitcast.4) | data formatting | bytes 322048

commit v4 on v3

v4 whole, which is shorter than its diff:
```python
import functools

import jax
import jax.numpy as jnp
from jax import lax
from jax.experimental import pallas as pl
from jax.experimental.pallas import tpu as pltpu
from jax.sharding import PartitionSpec as P

REACH = 4
LANES = 128
GROUP = 8
STEP_ROWS = 32
MESH = pl.DeviceIdType.MESH
F32 = jnp.float32
BF16 = jnp.bfloat16


def mm(left, right):
    return jnp.dot(left, right, preferred_element_type=F32)


def mm_last(left, right):
    return lax.dot_general(left, right, (((1,), (1,)), ((), ())), preferred_element_type=F32)


def iota(shape, dim):
    return lax.broadcasted_iota(jnp.int32, shape, dim)


def to_column(row, size):
    eye = iota((size, size), 0) == iota((size, size), 1)
    return jnp.sum(jnp.where(eye, row, 0.0), axis=1, keepdims=True)


def to_row(column, size):
    eye = iota((size, size), 0) == iota((size, size), 1)
    return jnp.sum(jnp.where(eye, column, 0.0), axis=0, keepdims=True)


def gate_parts(half):
    twice = jnp.tanh(half) + 1.0
    act = half * twice
    return act, twice + act * (2.0 - twice)


def kernel(
    n_tile, n_state, share_lo, share_hi,
    bands, slot_row, counties, table, label, w_first, taps, w_second, w_third, w_head,
    mean_out, grads_out,
    x_s, a1_s, a2_s, d1_s, d2_s, u3_s, u2_s, u1_s, slot_s, g_s, w2_s, w2t_s, w3_s, w3t_s, wh_s,
    acc_first, acc_second, acc_third, acc_head, first_lo, first_hi, second_s, third_s, tail,
    msg, msgs, flat_lo, flat_hi, parts_lo, parts_hi, zparts_lo, zparts_hi, whole_lo, whole_hi,
    x_sem, msg_send, msg_recv, *sum_sems,
):
    me = lax.axis_index("tile")
    my_state = lax.axis_index("state")
    c1, feat = w_first.shape
    c2 = w_second.shape[1]
    blocks = slot_row.shape[1]
    pixels = bands.shape[2]
    row_len = pixels // blocks
    cty_dev = label.shape[1]
    places = table.shape[1]
    slot_count = counties.shape[1]
    step_px = STEP_ROWS * row_len
    steps = pixels // step_px

    def band_copy(k):
        cols = pl.ds(pl.multiple_of(k * step_px, step_px), step_px)
        return pltpu.make_async_copy(bands.at[0, :, cols], x_s.at[:, cols], x_sem.at[k])

    for k in range(steps):
        band_copy(k).start()

    def tile_peer(by):
        return lax.rem(me + by + n_tile, n_tile)

    def state_peer(by):
        return lax.rem(my_state + by + n_state, n_state)

    barrier = pltpu.get_barrier_semaphore()
    for by in range(1, n_tile):
        pl.semaphore_signal(barrier, inc=1, device_id={"tile": tile_peer(by)}, device_id_type=MESH)
    for by in range(1, n_state):
        pl.semaphore_signal(
            barrier, inc=1, device_id={"state": state_peer(by)}, device_id_type=MESH
        )

    slots = slot_row[...].astype(F32)
    slot_s[...] = jnp.broadcast_to(to_column(slots, blocks), (blocks, LANES))
    half_second = w_second[...].astype(F32) * 0.5
    half_third = w_third[...].astype(F32) * 0.5
    w2t_s[...] = half_second.astype(BF16)
    w3_s[...] = half_third.astype(BF16)
    w2_s[...] = half_second.T.astype(BF16)
    w3t_s[...] = half_third.T.astype(BF16)
    head_row = w_head[...].astype(F32)
    wh_s[...] = jnp.broadcast_to(to_column(head_row, c2) * 0.5, (c2, LANES))
    tap_cols = [to_column(taps[k : k + 1, :], c1) for k in range(3)]
    lane = iota((c1, LANES), 1)
    tap_prev = jnp.where(lane == 0, 0.0, tap_cols[0] * 0.5)
    tap_here = jnp.broadcast_to(tap_cols[1] * 0.5, (c1, LANES))
    tap_next = jnp.where(lane == LANES - 1, 0.0, tap_cols[2] * 0.5)
    acc_first[...] = jnp.zeros_like(acc_first)
    acc_second[...] = jnp.zeros_like(acc_second)
    acc_third[...] = jnp.zeros_like(acc_third)
    acc_head[...] = jnp.zeros_like(acc_head)
    slot_ids = iota((2 * GROUP, LANES), 0).astype(F32)

    def row_cols(j):
        return slice(j * row_len, (j + 1) * row_len)

    def all_rows(tile):
        return jnp.concatenate([tile] * STEP_ROWS, axis=1)

    def forward(step, carry):
        band_copy(step).wait()
        cols = pl.ds(pl.multiple_of(step * step_px, step_px), step_px)
        h1 = mm(w_first[...], x_s[:, cols])
        s1 = []
        for j in range(STEP_ROWS):
            h = h1[:, row_cols(j)]
            s1.append(
                tap_prev * pltpu.roll(h, 1, 1)
                + tap_here * h
                + tap_next * pltpu.roll(h, LANES - 1, 1)
            )
        a1, d1 = gate_parts(jnp.concatenate(s1, axis=1))
        d1_s[:, cols] = d1
        a1 = a1.astype(BF16)
        a1_s[:, cols] = a1
        a2, d2 = gate_parts(mm(w2_s[...], a1))
        d2_s[:, cols] = d2
        a2 = a2.astype(BF16)
        a2_s[:, cols] = a2
        a3, d3 = gate_parts(mm(w3_s[...], a2))
        u3_s[:, cols] = (all_rows(wh_s[...]) * d3).astype(BF16)
        a3 = (a3 + a2.astype(F32)).astype(BF16)
        member = jnp.concatenate(
            [
                (slot_s[pl.ds(step * STEP_ROWS + j, 1), :] == slot_ids).astype(F32)
                for j in range(STEP_ROWS)
            ],
            axis=1,
        ).astype(BF16)
        acc_head[...] += mm_last(member, a3)
        return carry

    lax.fori_loop(0, steps, forward, 0)

    head_sums = acc_head[0:GROUP, :]
    slot_sums = jnp.sum(head_sums * head_row, axis=1, keepdims=True)
    in_slot = (slots == slot_ids[0:GROUP, :]).astype(F32)
    slot_counts = jnp.sum(in_slot, axis=1, keepdims=True) * float(row_len)
    county = to_column(counties[...].astype(F32), slot_count)
    hits = county == iota((slot_count, places), 1).astype(F32)
    place = jnp.sum(jnp.where(hits, table[...].astype(F32), 0.0), axis=1, keepdims=True)
    place = place - (me * cty_dev).astype(F32)
    place = jnp.where(place < 0.0, place + float(places), place)
    pick = (place == iota((slot_count, LANES), 1).astype(F32)).astype(F32)
    msg[...] = jnp.zeros_like(msg)
    msg[0:1, :] = jnp.sum(pick * slot_sums, axis=0, keepdims=True)
    msg[1:2, :] = jnp.sum(pick * slot_counts, axis=0, keepdims=True)
    msg[2:3, 0:cty_dev] = label[...].astype(F32)

    pl.semaphore_wait(barrier, n_tile - 1 + n_state - 1)
    offsets = [by for by in range(1 - REACH, REACH) if by]
    copies = []
    for n, by in enumerate(offsets):
        copies.append(
            pltpu.make_async_remote_copy(
                src_ref=msg,
                dst_ref=msgs.at[n],
                send_sem=msg_send.at[n],
                recv_sem=msg_recv.at[n],
                device_id={"tile": tile_peer(by)},
                device_id_type=MESH,
            )
        )
        copies[-1].start()

    def backward(step, carry):
        cols = pl.ds(pl.multiple_of(step * step_px, step_px), step_px)
        u2 = ((mm(w3t_s[...], u3_s[:, cols]) + all_rows(wh_s[...])) * d2_s[:, cols]).astype(BF16)
        u2_s[:, cols] = u2
        u1 = mm(w2t_s[...], u2) * d1_s[:, cols]
        left, right = [], []
        for j in range(STEP_ROWS):
            d = u1[:, row_cols(j)]
            left.append(jnp.where(lane == LANES - 1, 0.0, pltpu.roll(d, LANES - 1, 1)))
            right.append(jnp.where(lane == 0, 0.0, pltpu.roll(d, 1, 1)))
        u1_s[0:c1, cols] = jnp.concatenate(left, axis=1).astype(BF16)
        u1_s[c1 : 2 * c1, cols] = u1.astype(BF16)
        u1_s[2 * c1 : 3 * c1, cols] = jnp.concatenate(right, axis=1).astype(BF16)
        return carry

    lax.fori_loop(0, steps, backward, 0)

    total = msg[...]
    for n, by in enumerate(offsets):
        copies[n].wait_recv()
        total = total + pltpu.roll(msgs[n], (-by * cty_dev) % LANES, 1)
    for copy in copies:
        copy.wait_send()
    sums, counts, target = total[0:1, :], total[1:2, :], total[2:3, :] * 0.01
    denom = jnp.maximum(counts, 1.0)
    mean = sums / denom
    mean_out[...] = mean[:, 0:cty_dev]
    adjoint = jnp.where(
        counts > 0.5, 2.0 * (mean - target) / (float(n_tile * n_state) * denom), 0.0
    )
    slot_g = jnp.sum(jnp.where(pick > 0.5, adjoint, 0.0), axis=1, keepdims=True)
    slot_g = slot_g.astype(BF16).astype(F32)
    all_slots = slot_s[...]
    g_rows = jnp.zeros((blocks, LANES), F32)
    for s in range(slot_count):
        g_rows = jnp.where(all_slots == float(s), slot_g[s : s + 1, 0:1], g_rows)
    g_s[...] = g_rows

    def g_tile(step, chans):
        rows = []
        for j in range(STEP_ROWS):
            row = jnp.broadcast_to(g_s[pl.ds(step * STEP_ROWS + j, 1), :], (2 * GROUP, LANES))
            rows.append(jnp.concatenate([row.astype(BF16)] * (chans // (2 * GROUP)), axis=0))
        return jnp.concatenate(rows, axis=1)

    def deep_grads(step, carry):
        cols = pl.ds(pl.multiple_of(step * step_px, step_px), step_px)
        g = g_tile(step, c2)
        acc_third[...] += mm_last(u3_s[:, cols] * g, a2_s[:, cols])
        acc_second[...] += mm_last(u2_s[:, cols] * g, a1_s[:, cols])
        return carry

    def first_grads(step, carry):
        cols = pl.ds(pl.multiple_of(step * step_px, step_px), step_px)
        acc_first[...] += mm_last(u1_s[:, cols] * g_tile(step, 3 * c1), x_s[:, cols])
        return carry

    def summing(share, flat, parts, zparts, whole, part_send, part_recv, z_send, z_recv, all_send, all_recv):
        def share_of(index):
            return pl.ds(pl.multiple_of(index * share, share), share)

        scatter, across, gather = [], [], []
        for by in range(1, n_tile):
            peer = tile_peer(by)
            where = {"tile": peer}
            scatter.append(
                pltpu.make_async_remote_copy(
                    src_ref=flat.at[share_of(peer)],
                    dst_ref=parts.at[by - 1],
                    send_sem=part_send.at[by - 1],
                    recv_sem=part_recv.at[by - 1],
                    device_id=where,
                    device_id_type=MESH,
                )
            )
            gather.append(
                pltpu.make_async_remote_copy(
                    src_ref=whole.at[share_of(me)],
                    dst_ref=whole.at[share_of(me)],
                    send_sem=all_send.at[by - 1],
                    recv_sem=all_recv.at[by - 1],
                    device_id=where,
                    device_id_type=MESH,
                )
            )
        for by in range(1, n_state):
            across.append(
                pltpu.make_async_remote_copy(
                    src_ref=zparts.at[my_state],
                    dst_ref=zparts.at[my_state],
                    send_sem=z_send.at[by - 1],
                    recv_sem=z_recv.at[by - 1],
                    device_id={"state": state_peer(by)},
                    device_id_type=MESH,
                )
            )

        def first():
            for copy in scatter:
                copy.start()

        def second():
            piece = flat[share_of(me), :]
            for n, copy in enumerate(scatter):
                copy.wait_recv()
                piece = piece + parts[n]
            zparts[my_state] = piece
            for copy in across:
                copy.start()

        def third():
            for copy in across:
                copy.wait_recv()
            piece = zparts[0]
            for s in range(1, n_state):
                piece = piece + zparts[s]
            whole[share_of(me), :] = piece
            for copy in gather:
                copy.start()

        def last():
            for copy in gather:
                copy.wait_recv()
            for copy in scatter + across + gather:
                copy.wait_send()

        return first, second, third, last

    lo = summing(share_lo, flat_lo, parts_lo, zparts_lo, whole_lo, *sum_sems[0:6])
    hi = summing(share_hi, flat_hi, parts_hi, zparts_hi, whole_hi, *sum_sems[6:12])

    lax.fori_loop(0, steps, deep_grads, 0)

    base = c1 * feat // LANES
    half = LANES // 2
    d_head = jnp.sum(head_sums * slot_g, axis=0, keepdims=True)
    second_s[...] = jnp.zeros_like(second_s)
    second_s[0:c2, 0:half] = acc_second[...]
    third_s[0:c2, :] = acc_third[...]
    third_s[c2 : c2 + 1, :] = d_head
    second_s[c2 : c2 + 1, :] = third_s[0:1, :]
    one = iota((1, LANES), 1) < half
    tail[...] = jnp.zeros_like(tail)
    tail[1:2, :] = pltpu.roll(second_s[0:1, :], half, 1)
    odd = second_s[pl.ds(1, c2 // 2, stride=2), :]
    even = second_s[pl.ds(2, c2 // 2, stride=2), :]
    low = iota((c2 // 2, LANES), 1) < half
    tail[2 : 2 + c2 // 2, :] = jnp.where(low, odd, pltpu.roll(even, half, 1))
    start = 2 + c2 // 2
    low = iota((c2, LANES), 1) < half
    tail[start : start + c2, :] = jnp.where(
        low, pltpu.roll(third_s[0:c2, :], half, 1), pltpu.roll(third_s[1 : c2 + 1, :], half, 1)
    )
    tail[start + c2 : start + c2 + 1, :] = jnp.where(one, pltpu.roll(d_head, half, 1), 0.0)
    flat_hi[...] = tail[GROUP:, :]
    hi[0]()
    lax.fori_loop(0, steps // 2, first_grads, 0)
    hi[1]()
    lax.fori_loop(steps // 2, steps, first_grads, 0)
    hi[2]()

    g_first = [acc_first[k * c1 : (k + 1) * c1, :] for k in range(3)]
    weights = w_first[...].astype(F32)
    d_first = tap_cols[0] * g_first[0] + tap_cols[1] * g_first[1] + tap_cols[2] * g_first[2]
    tap_rows = [
        to_row(jnp.sum(weights * g, axis=1, keepdims=True), c1) for g in g_first
    ]
    first_lo[...] = d_first[:, 0:LANES]
    first_hi[:, 0 : feat - LANES] = d_first[:, LANES:feat]
    period = feat * GROUP // LANES
    groups = c1 // GROUP
    at = iota((groups, LANES), 1)
    flat_lo[...] = jnp.zeros_like(flat_lo)
    for j in range(period):
        chan, off = divmod(j * LANES, feat)
        lows = first_lo[pl.ds(chan, groups, stride=GROUP), :]
        highs = first_hi[pl.ds(chan, groups, stride=GROUP), :]
        value = pltpu.roll(highs, (-off) % LANES, 1)
        if off < LANES:
            shifted = pltpu.roll(lows, (-off) % LANES, 1) if off else lows
            value = jnp.where(at < LANES - off, shifted, value)
        if off + LANES > feat:
            after = first_lo[pl.ds(chan + 1, groups, stride=GROUP), :]
            value = jnp.where(at < feat - off, value, pltpu.roll(after, (feat - off) % LANES, 1))
        flat_lo[pl.ds(j, groups, stride=period), :] = value
    tail[0:1, :] = jnp.concatenate(tap_rows[0:2], axis=1)
    tail[1:2, :] = jnp.where(one, jnp.concatenate([tap_rows[2], tap_rows[2]], axis=1), tail[1:2, :])
    flat_lo[base : base + GROUP, :] = tail[0:GROUP, :]
    for phase in lo:
        phase()
    hi[3]()
    split = base + GROUP
    grads_out[0:split, :] = whole_lo[0:split, :]
    grads_out[split:, :] = whole_hi[...]


def on_device(
    n_tile, n_state,
    bands, block_slot, tile_counties, county_place, label, w_first, taps, w_second, w_third, w_head,
):
    feat, pixels = bands.shape[1:]
    c1, c2 = w_first.shape[0], w_second.shape[0]
    blocks = block_slot.shape[1]
    grads = c1 * feat + 3 * c1 + c2 * c1 + c2 * c2 + c2
    rows = pl.cdiv(grads, LANES)
    split = c1 * feat // LANES + GROUP
    share_lo = pl.cdiv(split, n_tile * GROUP) * GROUP
    share_hi = pl.cdiv(rows - split, n_tile * GROUP) * GROUP
    rows_lo, rows_hi = n_tile * share_lo, n_tile * share_hi
    steps = blocks // STEP_ROWS
    vmem = pl.BlockSpec(memory_space=pltpu.VMEM)
    dma = pltpu.SemaphoreType.DMA
    near = 2 * (REACH - 1)
    mean, out = pl.pallas_call(
        functools.partial(kernel, n_tile, n_state, share_lo, share_hi),
        out_shape=(
            jax.ShapeDtypeStruct(label.shape, F32),
            jax.ShapeDtypeStruct((split + rows_hi, LANES), F32),
        ),
        in_specs=[pl.BlockSpec(memory_space=pl.ANY)] + [vmem] * 9,
        out_specs=(vmem, vmem),
        scratch_shapes=[
            pltpu.VMEM((feat, pixels), BF16),
            pltpu.VMEM((c1, pixels), BF16),
            pltpu.VMEM((c2, pixels), BF16),
            pltpu.VMEM((c1, pixels), F32),
            pltpu.VMEM((c2, pixels), F32),
            pltpu.VMEM((c2, pixels), BF16),
            pltpu.VMEM((c2, pixels), BF16),
            pltpu.VMEM((3 * c1, pixels), BF16),
            pltpu.VMEM((blocks, LANES), F32),
            pltpu.VMEM((blocks, LANES), F32),
            pltpu.VMEM((c2, c1), BF16),
            pltpu.VMEM((c1, c2), BF16),
            pltpu.VMEM((c2, c2), BF16),
            pltpu.VMEM((c2, c2), BF16),
            pltpu.VMEM((c2, LANES), F32),
            pltpu.VMEM((3 * c1, feat), F32),
            pltpu.VMEM((c2, c1), F32),
            pltpu.VMEM((c2, c2), F32),
            pltpu.VMEM((2 * GROUP, c2), F32),
            pltpu.VMEM((c1, LANES), F32),
            pltpu.VMEM((c1, LANES), F32),
            pltpu.VMEM((c2 + GROUP, LANES), F32),
            pltpu.VMEM((c2 + GROUP, LANES), F32),
            pltpu.VMEM((GROUP + rows_hi, LANES), F32),
            pltpu.VMEM((GROUP, LANES), F32),
            pltpu.VMEM((near, GROUP, LANES), F32),
            pltpu.VMEM((rows_lo, LANES), F32),
            pltpu.VMEM((rows_hi, LANES), F32),
            pltpu.VMEM((n_tile - 1, share_lo, LANES), F32),
            pltpu.VMEM((n_tile - 1, share_hi, LANES), F32),
            pltpu.VMEM((n_state, share_lo, LANES), F32),
            pltpu.VMEM((n_state, share_hi, LANES), F32),
            pltpu.VMEM((rows_lo, LANES), F32),
            pltpu.VMEM((rows_hi, LANES), F32),
            dma((steps,)),
            dma((near,)),
            dma((near,)),
        ]
        + [
            dma((peers,))
            for peers in (n_tile - 1, n_tile - 1, n_state - 1, n_state - 1, n_tile - 1, n_tile - 1) * 2
        ],
        compiler_params=pltpu.CompilerParams(
            collective_id=0, has_side_effects=True, vmem_limit_bytes=56 * 2**20
        ),
    )(
        bands, block_slot, tile_counties, county_place, label,
        w_first, taps, w_second.T, w_third, w_head.reshape(1, -1),
    )
    return mean, out.reshape(-1)[:grads]


def solution(mesh):
    in_specs = (
        P("state", None, "tile"),
        P("state", "tile"),
        P("state", "tile"),
        P("state", None),
        P("state", "tile"),
        P(),
        P(),
        P(),
        P(),
        P(),
    )
    return jax.shard_map(
        functools.partial(on_device, mesh.shape["tile"], mesh.shape["state"]),
        mesh=mesh,
        in_specs=in_specs,
        out_specs=(P("state", "tile"), P()),
        check_vma=False,
    )
```

time: 45.3 us -> 44.7 us (0.987)
  Pallas kernels: 41.7 us -> 41.1 us
    pallas_call x1, Pallas kernels: 41.7 us -> 41.1 us  [on_device(): pl.pallas_call(functools.partial(kernel, n_tile, n_state, share_lo, share...]
where the time goes in v4:
time: 44.7 us; the launch traced here: 44.4 us
  Pallas kernels  41.1 us (92%)
  local copies, waits for them, and re-layouts  2.73 us (6%)
  between operations  0.64 us (1%)
    pallas_call x1, Pallas kernels, on_device(): pl.pallas_call(functools.partial(kernel, n_tile, n_state, share_lo, share...  41.1 us
    unnamed x2, local copies, waits for them, and re-layouts  2.73 us

profile of v4, /device:TPU:0, one launch (start us, length us, event | category | flops | bytes accessed | tf_op | source)
XLA Modules:
  0.0 44.4 jit_solution(11533844636064695663)
XLA Ops:
  0.6 41.1 %shard_map.113 = (f32[1,12]{1,0:T(1,128)}, f32[320,128]{1,0:T(8,128)}) custom-call(bf16[1,240,16384]{2,1,0:T(8,128)(2,1)} %bands.1, s32[1,128]{1,0:T(1,128)} %slot_row.1, s32[1,8]{1,0:T(1,128)} %counties.1, s32[1,96]{1,0:T(1,128)} %table.1, s32[1,12]{1,0:T(1,128)} %label.1, bf16[64,240]{1,0:T(8,128)(2,1)} %w_first.1, f32[3,64]{1,0:T(4,128)} %taps.1, ...), custom_call_target="tpu_custom_call" | custom-call | tf_op jit(solution)/shard_map/pallas_call | solution.py:396
  41.7 1.1 %copy.14 = f32[1,12]{1,0:T(1,128)} copy(f32[1,12]{1,0:T(1,128)} %get-tuple-element.8) | data formatting | bytes 96
  42.9 1.6 %copy.15 = f32[40256]{0:T(1024)} copy(f32[40256]{0:T(1024)} %bitcast.4) | data formatting | bytes 322048

commit v5 on v4

--- a/solution.py
+++ b/solution.py
@@ -11,6 +11,8 @@
 LANES = 128
 GROUP = 8
 STEP_ROWS = 32
+TICK_ROWS = 2
+SUM_ROWS = 8
 MESH = pl.DeviceIdType.MESH
 F32 = jnp.float32
 BF16 = jnp.bfloat16
@@ -111,40 +113,77 @@
     def row_cols(j):
         return slice(j * row_len, (j + 1) * row_len)
 
-    def all_rows(tile):
-        return jnp.concatenate([tile] * STEP_ROWS, axis=1)
+    ticks = STEP_ROWS // TICK_ROWS
+    tick_px = TICK_ROWS * row_len
+
+    def columns(step, tick, j=None):
+        first = step * step_px + tick * tick_px + (0 if j is None else j * row_len)
+        size = tick_px if j is None else row_len
+        return pl.ds(pl.multiple_of(first, row_len), size)
+
+    def skewed(stages):
+        held = [None] * len(stages)
+        for now in range(ticks + len(stages) - 1):
+            for n in reversed(range(len(stages))):
+                tick = now - n
+                if 0 <= tick < ticks:
+                    held[n] = stages[n](tick, held[n - 1] if n else None)
+
+    def halves():
+        return [slice(r, r + c1) for r in range(0, c2, c1)]
 
     def forward(step, carry):
         band_copy(step).wait()
-        cols = pl.ds(pl.multiple_of(step * step_px, step_px), step_px)
-        h1 = mm(w_first[...], x_s[:, cols])
-        s1 = []
-        for j in range(STEP_ROWS):
-            h = h1[:, row_cols(j)]
-            s1.append(
-                tap_prev * pltpu.roll(h, 1, 1)
-                + tap_here * h
-                + tap_next * pltpu.roll(h, LANES - 1, 1)
+        head = [acc_head[...]]
+
+        def stage_one(tick, _):
+            return mm(w_first[...], x_s[:, columns(step, tick)])
+
+        def stage_two(tick, h1):
+            tiles = []
+            for j in range(TICK_ROWS):
+                h = h1[:, row_cols(j)]
+                s1 = (
+                    tap_prev * pltpu.roll(h, 1, 1)
+                    + tap_here * h
+                    + tap_next * pltpu.roll(h, LANES - 1, 1)
+                )
+                act, d1_s[:, columns(step, tick, j)] = gate_parts(s1)
+                act = act.astype(BF16)
+                a1_s[:, columns(step, tick, j)] = act
+                tiles.append(act)
+            return mm(w2_s[...], jnp.concatenate(tiles, axis=1))
+
+        def stage_three(tick, h2):
+            tiles = []
+            for j in range(TICK_ROWS):
+                parts = []
+                for part in halves():
+                    act, d2_s[part, columns(step, tick, j)] = gate_parts(h2[part, row_cols(j)])
+                    act = act.astype(BF16)
+                    a2_s[part, columns(step, tick, j)] = act
+                    parts.append(act)
+                tiles.append(jnp.concatenate(parts, axis=0))
+            return mm(w3_s[...], jnp.concatenate(tiles, axis=1))
+
+        def stage_four(tick, h3):
+            tiles, members = [], []
+            for j in range(TICK_ROWS):
+                parts = []
+                for part in halves():
+                    act, d3 = gate_parts(h3[part, row_cols(j)])
+                    u3_s[part, columns(step, tick, j)] = (wh_s[part, :] * d3).astype(BF16)
+                    a2 = a2_s[part, columns(step, tick, j)].astype(F32)
+                    parts.append((act + a2).astype(BF16))
+                tiles.append(jnp.concatenate(parts, axis=0))
+                row = slot_s[pl.ds(step * STEP_ROWS + tick * TICK_ROWS + j, 1), :]
+                members.append((row == slot_ids).astype(F32).astype(BF16))
+            head[0] = head[0] + mm_last(
+                jnp.concatenate(members, axis=1), jnp.concatenate(tiles, axis=1)
             )
-        a1, d1 = gate_parts(jnp.concatenate(s1, axis=1))
-        d1_s[:, cols] = d1
-        a1 = a1.astype(BF16)
-        a1_s[:, cols] = a1
-        a2, d2 = gate_parts(mm(w2_s[...], a1))
-        d2_s[:, cols] = d2
-        a2 = a2.astype(BF16)
-        a2_s[:, cols] = a2
-        a3, d3 = gate_parts(mm(w3_s[...], a2))
-        u3_s[:, cols] = (all_rows(wh_s[...]) * d3).astype(BF16)
-        a3 = (a3 + a2.astype(F32)).astype(BF16)
-        member = jnp.concatenate(
-            [
-                (slot_s[pl.ds(step * STEP_ROWS + j, 1), :] == slot_ids).astype(F32)
-                for j in range(STEP_ROWS)
-            ],
-            axis=1,
-        ).astype(BF16)
-        acc_head[...] += mm_last(member, a3)
+
+        skewed([stage_one, stage_two, stage_three, stage_four])
+        acc_head[...] = head[0]
         return carry
 
     lax.fori_loop(0, steps, forward, 0)
@@ -181,18 +220,34 @@
         copies[-1].start()
 
     def backward(step, carry):
-        cols = pl.ds(pl.multiple_of(step * step_px, step_px), step_px)
-        u2 = ((mm(w3t_s[...], u3_s[:, cols]) + all_rows(wh_s[...])) * d2_s[:, cols]).astype(BF16)
-        u2_s[:, cols] = u2
-        u1 = mm(w2t_s[...], u2) * d1_s[:, cols]
-        left, right = [], []
-        for j in range(STEP_ROWS):
-            d = u1[:, row_cols(j)]
-            left.append(jnp.where(lane == LANES - 1, 0.0, pltpu.roll(d, LANES - 1, 1)))
-            right.append(jnp.where(lane == 0, 0.0, pltpu.roll(d, 1, 1)))
-        u1_s[0:c1, cols] = jnp.concatenate(left, axis=1).astype(BF16)
-        u1_s[c1 : 2 * c1, cols] = u1.astype(BF16)
-        u1_s[2 * c1 : 3 * c1, cols] = jnp.concatenate(right, axis=1).astype(BF16)
+        def stage_one(tick, _):
+            return mm(w3t_s[...], u3_s[:, columns(step, tick)])
+
+        def stage_two(tick, d_a2):
+            tiles = []
+            for j in range(TICK_ROWS):
+                parts = []
+                for part in halves():
+                    d_h2 = (d_a2[part, row_cols(j)] + wh_s[part, :]) * d2_s[part, columns(step, tick, j)]
+                    d_h2 = d_h2.astype(BF16)
+                    u2_s[part, columns(step, tick, j)] = d_h2
+                    parts.append(d_h2)
+                tiles.append(jnp.concatenate(parts, axis=0))
+            return mm(w2t_s[...], jnp.concatenate(tiles, axis=1))
+
+        def stage_three(tick, d_a1):
+            for j in range(TICK_ROWS):
+                cols = columns(step, tick, j)
+                d = d_a1[:, row_cols(j)] * d1_s[:, cols]
+                u1_s[0:c1, cols] = jnp.where(
+                    lane == LANES - 1, 0.0, pltpu.roll(d, LANES - 1, 1)
+                ).astype(BF16)
+                u1_s[c1 : 2 * c1, cols] = d.astype(BF16)
+                u1_s[2 * c1 : 3 * c1, cols] = jnp.where(lane == 0, 0.0, pltpu.roll(d, 1, 1)).astype(
+                    BF16
+                )
+
+        skewed([stage_one, stage_two, stage_three])
         return carry
 
     lax.fori_loop(0, steps, backward, 0)
@@ -218,23 +273,33 @@
         g_rows = jnp.where(all_slots == float(s), slot_g[s : s + 1, 0:1], g_rows)
     g_s[...] = g_rows
 
-    def g_tile(step, chans):
-        rows = []
-        for j in range(STEP_ROWS):
-            row = jnp.broadcast_to(g_s[pl.ds(step * STEP_ROWS + j, 1), :], (2 * GROUP, LANES))
-            rows.append(jnp.concatenate([row.astype(BF16)] * (chans // (2 * GROUP)), axis=0))
-        return jnp.concatenate(rows, axis=1)
+    def scaled(field, first):
+        tiles = []
+        for j in range(SUM_ROWS):
+            row = jnp.broadcast_to(g_s[pl.ds(first + j, 1), :], (2 * GROUP, LANES)).astype(BF16)
+            tile = jnp.concatenate([row] * (field.shape[0] // (2 * GROUP)), axis=0)
+            cols = pl.ds(pl.multiple_of((first + j) * row_len, row_len), row_len)
+            tiles.append(field[:, cols] * tile)
+        return jnp.concatenate(tiles, axis=1)
+
+    def chunks(step):
+        for n in range(STEP_ROWS // SUM_ROWS):
+            first = step * STEP_ROWS + n * SUM_ROWS
+            px = SUM_ROWS * row_len
+            yield first, pl.ds(pl.multiple_of(first * row_len, px), px)
 
     def deep_grads(step, carry):
-        cols = pl.ds(pl.multiple_of(step * step_px, step_px), step_px)
-        g = g_tile(step, c2)
-        acc_third[...] += mm_last(u3_s[:, cols] * g, a2_s[:, cols])
-        acc_second[...] += mm_last(u2_s[:, cols] * g, a1_s[:, cols])
+        third, second = acc_third[...], acc_second[...]
+        for first, cols in chunks(step):
+            third = third + mm_last(scaled(u3_s, first), a2_s[:, cols])
+            second = second + mm_last(scaled(u2_s, first), a1_s[:, cols])
+        acc_third[...] = third
+        acc_second[...] = second
         return carry
 
     def first_grads(step, carry):
-        cols = pl.ds(pl.multiple_of(step * step_px, step_px), step_px)
-        acc_first[...] += mm_last(u1_s[:, cols] * g_tile(step, 3 * c1), x_s[:, cols])
+        for first, cols in chunks(step):
+            acc_first[...] += mm_last(scaled(u1_s, first), x_s[:, cols])
         return carry
 
     def summing(share, flat, parts, zparts, whole, part_send, part_recv, z_send, z_recv, all_send, all_recv):

time: 44.7 us -> 61.1 us (1.37)
  Pallas kernels: 41.1 us -> 57.5 us
    pallas_call x1, Pallas kernels: 41.1 us -> 57.5 us  [on_device(): pl.pallas_call(functools.partial(kernel, n_tile, n_state, share_lo, share...]
where the time goes in v5:
time: 61.1 us; the launch traced here: 60.8 us
  Pallas kernels  57.5 us (94%)
  local copies, waits for them, and re-layouts  2.73 us (4%)
  between operations  0.64 us (1%)
    pallas_call x1, Pallas kernels, on_device(): pl.pallas_call(functools.partial(kernel, n_tile, n_state, share_lo, share...  57.5 us
    unnamed x2, local copies, waits for them, and re-layouts  2.73 us

profile of v5, /device:TPU:0, one launch (start us, length us, event | category | flops | bytes accessed | tf_op | source)
XLA Modules:
  0.0 60.8 jit_solution(7891318465016199008)
XLA Ops:
  0.6 57.5 %shard_map.113 = (f32[1,12]{1,0:T(1,128)}, f32[320,128]{1,0:T(8,128)}) custom-call(bf16[1,240,16384]{2,1,0:T(8,128)(2,1)} %bands.1, s32[1,128]{1,0:T(1,128)} %slot_row.1, s32[1,8]{1,0:T(1,128)} %counties.1, s32[1,96]{1,0:T(1,128)} %table.1, s32[1,12]{1,0:T(1,128)} %label.1, bf16[64,240]{1,0:T(8,128)(2,1)} %w_first.1, f32[3,64]{1,0:T(4,128)} %taps.1, ...), custom_call_target="tpu_custom_call" | custom-call | tf_op jit(solution)/shard_map/pallas_call | solution.py:461
  58.1 1.1 %copy.14 = f32[1,12]{1,0:T(1,128)} copy(f32[1,12]{1,0:T(1,128)} %get-tuple-element.8) | data formatting | bytes 96
  59.2 1.6 %copy.15 = f32[40256]{0:T(1024)} copy(f32[40256]{0:T(1024)} %bitcast.4) | data formatting | bytes 322048

commit v6 on v5

--- a/solution.py
+++ b/solution.py
@@ -11,8 +11,8 @@
 LANES = 128
 GROUP = 8
 STEP_ROWS = 32
-TICK_ROWS = 2
-SUM_ROWS = 8
+TICK_ROWS = 16
+SUM_ROWS = 32
 MESH = pl.DeviceIdType.MESH
 F32 = jnp.float32
 BF16 = jnp.bfloat16
@@ -164,17 +164,18 @@
                     a2_s[part, columns(step, tick, j)] = act
                     parts.append(act)
                 tiles.append(jnp.concatenate(parts, axis=0))
-            return mm(w3_s[...], jnp.concatenate(tiles, axis=1))
-
-        def stage_four(tick, h3):
+            tiles = jnp.concatenate(tiles, axis=1)
+            return mm(w3_s[...], tiles), tiles
+
+        def stage_four(tick, before):
+            h3, a2 = before
             tiles, members = [], []
             for j in range(TICK_ROWS):
                 parts = []
                 for part in halves():
                     act, d3 = gate_parts(h3[part, row_cols(j)])
                     u3_s[part, columns(step, tick, j)] = (wh_s[part, :] * d3).astype(BF16)
-                    a2 = a2_s[part, columns(step, tick, j)].astype(F32)
-                    parts.append((act + a2).astype(BF16))
+                    parts.append((act + a2[part, row_cols(j)].astype(F32)).astype(BF16))
                 tiles.append(jnp.concatenate(parts, axis=0))
                 row = slot_s[pl.ds(step * STEP_ROWS + tick * TICK_ROWS + j, 1), :]
                 members.append((row == slot_ids).astype(F32).astype(BF16))

time: 61.1 us -> 48.2 us (0.79)
  Pallas kernels: 57.5 us -> 44.6 us
    pallas_call x1, Pallas kernels: 57.5 us -> 44.6 us  [on_device(): pl.pallas_call(functools.partial(kernel, n_tile, n_state, share_lo, share...]
where the time goes in v6:
time: 48.2 us; the launch traced here: 48 us
  Pallas kernels  44.6 us (93%)
  local copies, waits for them, and re-layouts  2.73 us (6%)
  between operations  0.64 us (1%)
    pallas_call x1, Pallas kernels, on_device(): pl.pallas_call(functools.partial(kernel, n_tile, n_state, share_lo, share...  44.6 us
    unnamed x2, local copies, waits for them, and re-layouts  2.73 us

profile of v6, /device:TPU:0, one launch (start us, length us, event | category | flops | bytes accessed | tf_op | source)
XLA Modules:
  0.0 48.0 jit_solution(7940056642335423980)
XLA Ops:
  0.6 44.6 %shard_map.113 = (f32[1,12]{1,0:T(1,128)}, f32[320,128]{1,0:T(8,128)}) custom-call(bf16[1,240,16384]{2,1,0:T(8,128)(2,1)} %bands.1, s32[1,128]{1,0:T(1,128)} %slot_row.1, s32[1,8]{1,0:T(1,128)} %counties.1, s32[1,96]{1,0:T(1,128)} %table.1, s32[1,12]{1,0:T(1,128)} %label.1, bf16[64,240]{1,0:T(8,128)(2,1)} %w_first.1, f32[3,64]{1,0:T(4,128)} %taps.1, ...), custom_call_target="tpu_custom_call" | custom-call | tf_op jit(solution)/shard_map/pallas_call | solution.py:462
  45.3 1.1 %copy.14 = f32[1,12]{1,0:T(1,128)} copy(f32[1,12]{1,0:T(1,128)} %get-tuple-element.8) | data formatting | bytes 96
  46.4 1.6 %copy.15 = f32[40256]{0:T(1024)} copy(f32[40256]{0:T(1024)} %bitcast.4) | data formatting | bytes 322048

commit v7 on v3

--- a/solution.py
+++ b/solution.py
@@ -10,8 +10,8 @@
 REACH = 4
 LANES = 128
 GROUP = 8
-STEP_ROWS = 16
-DMA_STEPS = 8
+STEP_ROWS = 32
+DMA_STEPS = 4
 MESH = pl.DeviceIdType.MESH
 F32 = jnp.float32
 BF16 = jnp.bfloat16

time: 45.3 us -> 42.6 us (0.940)
  Pallas kernels: 41.7 us -> 39 us
    pallas_call x1, Pallas kernels: 41.7 us -> 39 us  [on_device(): pl.pallas_call(functools.partial(kernel, n_tile, n_state, share), out_sha...]
where the time goes in v7:
time: 42.6 us; the launch traced here: 42.4 us
  Pallas kernels  39 us (92%)
  local copies, waits for them, and re-layouts  2.73 us (6%)
  between operations  0.64 us (2%)
    pallas_call x1, Pallas kernels, on_device(): pl.pallas_call(functools.partial(kernel, n_tile, n_state, share), out_sha...  39 us
    unnamed x2, local copies, waits for them, and re-layouts  2.73 us

profile of v7, /device:TPU:0, one launch (start us, length us, event | category | flops | bytes accessed | tf_op | source)
XLA Modules:
  0.0 42.4 jit_solution(7696208301727665844)
XLA Ops:
  0.6 39.0 %shard_map.113 = (f32[1,12]{1,0:T(1,128)}, f32[320,128]{1,0:T(8,128)}) custom-call(bf16[1,240,16384]{2,1,0:T(8,128)(2,1)} %bands.1, s32[1,128]{1,0:T(1,128)} %slot_row.1, s32[1,8]{1,0:T(1,128)} %counties.1, s32[1,96]{1,0:T(1,128)} %table.1, s32[1,12]{1,0:T(1,128)} %label.1, bf16[64,240]{1,0:T(8,128)(2,1)} %w_first.1, f32[3,64]{1,0:T(4,128)} %taps.1, ...), custom_call_target="tpu_custom_call" | custom-call | tf_op jit(solution)/shard_map/pallas_call | solution.py:364
  39.7 1.1 %copy.14 = f32[1,12]{1,0:T(1,128)} copy(f32[1,12]{1,0:T(1,128)} %get-tuple-element.8) | data formatting | bytes 96
  40.8 1.6 %copy.15 = f32[40256]{0:T(1024)} copy(f32[40256]{0:T(1024)} %bitcast.4) | data formatting | bytes 322048
